TPU v7x, 256 devices: a whole 4x4x8 slice. The times are simulated.
256 devices in a mesh: segment: 2 (over core), tile: 128 (over x, y, z).
Axes of the slice: x: 4, y: 4, z: 8, core: 2. Of those that a mesh axis runs over, the one named last changes fastest.
Arguments:
- inputs: bfloat16 [2, 1024, 8, 256], P(None, 'tile'), may hold values from -6 to 6
- cotangent: bfloat16 [2, 1024, 8, 256], P(None, 'tile'), may hold values from -6 to 6
- side_owner: int32 [128, 4], replicated, may hold values from 0 to 127, as said below
- side_from: int32 [128, 4], replicated, may hold values from 0 to 3
- corner_from: int32 [128, 4], replicated, may hold values from 0 to 3
- corner_live: int32 [128, 4], replicated, may hold values 0 or 1
- depth_kernel: bfloat16 [4, 49, 256], P('segment'), may hold values from -0.875 to 0.875
- norm_gain: float32 [4, 256], P('segment'), may hold values from 0.1 to 1.9
- in_weight: bfloat16 [4, 256, 1024], P('segment'), may hold values from -0.375 to 0.375
- out_weight: bfloat16 [4, 1024, 256], P('segment'), may hold values from -0.1875 to 0.1875
- layer_scale: float32 [4, 256], P('segment'), may hold values from 0.1 to 1.9
Outputs:
- input_grads: bfloat16 [2, 1024, 8, 256], P('segment', 'tile')
- grad_kernel: float32 [4, 49, 256], P('segment')
- grad_gain: float32 [4, 256], P('segment')
- grad_in: float32 [4, 256, 1024], P('segment')
- grad_out: float32 [4, 1024, 256], P('segment')
- grad_scale: float32 [4, 256], P('segment')
Inputs may be any that keep to these rules, and one draw needn't show every extreme that they name: side_owner[t,0] is t - 8 or t - 7, side_owner[t,1] is t + 1, side_owner[t,2] is t + 8 or t + 7, side_owner[t,3] is t - 1, all modulo 128.
All inputs are finite; a program needn't handle non-finite values.
Results may differ from a plain program's by a relative error of at most 0.024.
Values may be sent and summed in bfloat16 or wider, within the bound.
A program may use at most 128 MiB of HBM per device.

v0:
```python
import functools

import jax
import jax.numpy as jnp
from jax import lax
from jax.experimental import pallas as pl
from jax.experimental.pallas import tpu as pltpu
from jax.sharding import PartitionSpec as P

GW = 8
BLOCKS = 4
C = 256
HID = 1024
EPSILON = 1e-06
ROOT_HALF = 0.7071067811865476
INV_ROOT_TAU = 0.3989422804014327
MESH = pl.DeviceIdType.MESH
F32 = jnp.float32
BF16 = jnp.bfloat16

OFFSETS = (-1, 1, -GW - 1, -GW, -GW + 1, -GW + 2, GW + 1, GW, GW - 1, GW - 2)
ROWS = (32, 32, 16, 32, 32, 16, 16, 32, 32, 16)
BASE = (0, 32, 192, 64, 96, 208, 224, 128, 160, 240)
SEND_ORDER = (2, 5, 6, 9, 3, 4, 7, 8, 0, 1)
SMALL = 56


def dot(a, b, da=1, db=0):
    return lax.dot_general(a, b, (((da,), (db,)), ((), ())), preferred_element_type=F32)


def pick(code, values):
    out = jnp.int32(values[-1])
    for k in range(len(values) - 2, -1, -1):
        out = jnp.where(code == k, jnp.int32(values[k]), out)
    return out


def seam_steps(so, t, n):
    north = lax.rem(so[t, 0] - t + GW + n, n)
    south = lax.rem(t + GW - so[t, 2] + n, n)
    return north, south


def wanted_rim(slot, t, so, sf, cf, n):
    north, south = seam_steps(so, t, n)
    if slot == 0:
        return sf[t, 3]
    if slot == 1:
        return sf[t, 1]
    if slot == 2:
        return cf[t, 0]
    if slot == 3:
        return jnp.where(north == 0, sf[t, 0], cf[t, 0])
    if slot == 4:
        return jnp.where(north == 1, sf[t, 0], cf[t, 1])
    if slot == 5:
        return cf[t, 1]
    if slot == 6:
        return cf[t, 2]
    if slot == 7:
        return jnp.where(south == 0, sf[t, 2], cf[t, 2])
    if slot == 8:
        return jnp.where(south == 1, sf[t, 2], cf[t, 3])
    return cf[t, 3]


def send_matrix(me, n, so, sf, cf):
    parts = [None] * 10
    for slot in range(10):
        rows = ROWS[slot]
        code = wanted_rim(slot, lax.rem(me - OFFSETS[slot] + n, n), so, sf, cf, n)
        a = pick(code, (0, 7, 63, 56))
        b = pick(code, (8, -1, -8, 1))
        d = pick(code, (1, 8, -1, -8))
        row = lax.broadcasted_iota(jnp.int32, (rows, 64), 0)
        pixel = lax.broadcasted_iota(jnp.int32, (rows, 64), 1)
        if rows == 32:
            i, j = row >> 3, row & 7
            valid = row < 24
        else:
            i, j = row >> 2, row & 3
            valid = (row < 12) & (j < 3)
        hit = (pixel == a + b * i + d * j) & valid
        parts[slot] = jnp.where(hit, 1.0, 0.0).astype(F32)
    order = sorted(range(10), key=lambda s: BASE[s])
    return jnp.concatenate([parts[s] for s in order], axis=0)


def place_matrix(me, n, so, cl):
    north, south = seam_steps(so, me, n)
    nz, sz = north == 0, south == 0

    def base(zero, slot_a, slot_b):
        return jnp.where(zero, jnp.int32(BASE[slot_a]), jnp.int32(BASE[slot_b]))

    def step(zero, slot_a, slot_b):
        return jnp.where(
            zero, jnp.int32(8 if ROWS[slot_a] == 32 else 4), jnp.int32(8 if ROWS[slot_b] == 32 else 4)
        )

    x = lax.broadcasted_iota(jnp.int32, (16, 256), 0)
    lane = lax.broadcasted_iota(jnp.int32, (16, 256), 1)
    live = [cl[me, c] == 1 for c in range(4)]

    def corner(c, i, j):
        zero, sa, sb = ((nz, 2, 3), (nz, 4, 5), (sz, 6, 7), (sz, 8, 9))[c]
        col = base(zero, sa, sb) + i * step(zero, sa, sb) + j
        return jnp.where(live[c], col, -1)

    blocks = []
    for y in range(14):
        if y < 3:
            left = corner(0, 2 - y, 2 - x)
            mid = base(nz, 3, 4) + (2 - y) * 8 + 10 - x
            right = corner(1, x - 11, 2 - y)
        elif y < 11:
            left = BASE[0] + (2 - x) * 8 + y - 3
            mid = jnp.full_like(x, -1)
            right = BASE[1] + (x - 11) * 8 + 10 - y
        else:
            left = corner(3, 2 - x, y - 11)
            mid = base(sz, 7, 8) + (y - 11) * 8 + x - 3
            right = corner(2, y - 11, x - 11)
        col = jnp.where(x < 3, left, jnp.where(x < 11, mid, jnp.where(x < 14, right, -1)))
        blocks.append(jnp.where(lane == col, 1.0, 0.0).astype(F32))
    blocks.append(jnp.zeros((32, 256), F32))
    return jnp.concatenate(blocks, axis=0)


def whole_wait(ref, sem):
    pltpu.make_async_copy(ref, ref, sem).wait()


def kernel(
    n,
    xin, cot, so, sf, cf, cl, dk, ng, ls, win_in, wout_in,
    dx_out, g_out, small_out,
    win, wout, pk, s_m, st_m, p_m, pt_m,
    pad, dpad, normed_s, inv_s, mixed_s, before_s, slope_s,
    u_s, h_s, dm_s, db_s, pa, pb,
    send_f, recv_f, send_b, recv_b,
    wsem, wsend, pksem, fs_sem, fr_sem, bs_sem, br_sem, psend, precv,
):
    seg = lax.axis_index("segment")
    me = lax.axis_index("tile")
    other = 1 - seg

    for l in range(2):
        b = 2 * seg + l
        pltpu.make_async_copy(win_in.at[l], win.at[b], wsem.at[0, b]).start()
        pltpu.make_async_copy(wout_in.at[l], wout.at[b], wsem.at[1, b]).start()

    barrier = pltpu.get_barrier_semaphore()
    for off in OFFSETS:
        pl.semaphore_signal(
            barrier, inc=1, device_id=(seg, lax.rem(me - off + n, n)), device_id_type=MESH
        )
    pl.semaphore_signal(barrier, inc=1, device_id=(other, me), device_id_type=MESH)

    for l in range(2):
        b = 2 * seg + l
        pk[b, 0:49, :] = dk[l].astype(F32)
        pk[b, 49:50, :] = ng[l : l + 1, :]
        pk[b, 50:51, :] = ls[l : l + 1, :]
        pk[b, 51:56, :] = jnp.zeros((5, C), F32)
    s_f = send_matrix(me, n, so, sf, cf)
    s_m[...] = s_f.astype(BF16)
    curb = xin[seg]
    send_f[0] = dot(s_m[...], curb).astype(BF16)

    pl.semaphore_wait(barrier, len(OFFSETS) + 1)

    def exchange(src, dst, ssem, rsem, sign):
        for slot in SEND_ORDER:
            rows = pl.ds(BASE[slot], ROWS[slot])
            pltpu.make_async_remote_copy(
                src_ref=src.at[rows],
                dst_ref=dst.at[rows],
                send_sem=ssem,
                recv_sem=rsem,
                device_id=(seg, lax.rem(me - sign * OFFSETS[slot] + n, n)),
                device_id_type=MESH,
            ).start()

    def to_partner(src, dst, ssem, rsem):
        return pltpu.make_async_remote_copy(
            src_ref=src, dst_ref=dst, send_sem=ssem, recv_sem=rsem,
            device_id=(other, me), device_id_type=MESH,
        )

    exchange(send_f.at[0], recv_f.at[0], fs_sem.at[0], fr_sem.at[0], 1)
    mine = pl.ds(2 * seg, 2)
    pk_copy = to_partner(pk.at[mine], pk.at[mine], pksem.at[0], pksem.at[1])
    pk_copy.start()
    w_copies = []
    for l in range(2):
        b = 2 * seg + l
        w_copies.append(to_partner(win_in.at[l], win.at[b], wsend.at[0, l], wsem.at[0, b]))
        w_copies.append(to_partner(wout_in.at[l], wout.at[b], wsend.at[1, l], wsem.at[1, b]))
    for copy in w_copies:
        copy.start()

    st_m[...] = jnp.transpose(s_f).astype(BF16)
    p_f = place_matrix(me, n, so, cl)
    p_m[...] = p_f.astype(BF16)
    pt_m[...] = jnp.transpose(p_f).astype(BF16)
    pk_copy.wait()

    def slope_of(b):
        before = before_s[...]
        slope_s[b] = (
            0.5 * (1.0 + lax.erf(before * ROOT_HALF))
            + before * jnp.exp(-0.5 * before * before) * INV_ROOT_TAU
        )

    for b in range(BLOCKS):
        if b > 0:
            send_f[b] = dot(s_m[...], curb).astype(BF16)
            exchange(send_f.at[b], recv_f.at[b], fs_sem.at[b], fr_sem.at[b], 1)
            slope_of(b - 1)
        cur = curb.astype(F32)
        whole_wait(recv_f.at[b], fr_sem.at[b])
        pad[b] = dot(p_m[...], recv_f[b]).reshape(16, 16, C)
        pad[b, 3:11, 3:11, :] = cur.reshape(8, 8, C)
        acc = jnp.zeros((8, 8, C), F32)
        for q in range(7):
            cols = pad[b, 0:14, q : q + 8, :]
            for r in range(7):
                acc = acc + cols[r : r + 8] * pk[b, 7 * r + q : 7 * r + q + 1, :]
        filtered = acc.reshape(64, C)
        centred = filtered - jnp.mean(filtered, axis=-1, keepdims=True)
        inv_std = lax.rsqrt(jnp.mean(centred * centred, axis=-1, keepdims=True) + EPSILON)
        normed = centred * inv_std
        normed_s[b] = normed
        inv_s[b] = jnp.broadcast_to(inv_std, (64, 128))
        unit = (normed * pk[b, 49:50, :]).astype(BF16)
        u_s[b] = unit
        whole_wait(win.at[b], wsem.at[0, b])
        before = dot(unit, win[b])
        before_s[...] = before
        hidden = (0.5 * before * (1.0 + lax.erf(before * ROOT_HALF))).astype(BF16)
        h_s[b] = hidden
        whole_wait(wout.at[b], wsem.at[1, b])
        mixed = dot(hidden, wout[b])
        mixed_s[b] = mixed
        curb = (cur + pk[b, 50:51, :] * mixed).astype(BF16)

        @pl.when(seg == 0)
        def _():
            to_partner(h_s.at[b], pb.at[b], psend.at[0, b], precv.at[1, b]).start()

        @pl.when(seg == 1)
        def _():
            to_partner(u_s.at[b], pa.at[b], psend.at[0, b], precv.at[0, b]).start()

    up = cot[seg].astype(F32)
    slope_of(BLOCKS - 1)
    for b in reversed(range(BLOCKS)):
        dm = (up * pk[b, 50:51, :]).astype(BF16)
        dm_s[b] = dm

        @pl.when(seg == 0)
        def _():
            to_partner(dm_s.at[b], pa.at[b], psend.at[1, b], precv.at[0, b]).start()

        d_hidden = dot(dm, wout[b], 1, 1)
        db = (d_hidden * slope_s[b]).astype(BF16)
        db_s[b] = db

        @pl.when(seg == 1)
        def _():
            to_partner(db_s.at[b], pb.at[b], psend.at[1, b], precv.at[1, b]).start()

        d_unit = dot(db, win[b], 1, 1)
        normed = normed_s[b]
        inv_std = inv_s[b, :, 0:1]
        dn = d_unit * pk[b, 49:50, :]
        df = inv_std * (
            dn
            - jnp.mean(dn, axis=-1, keepdims=True)
            - normed * jnp.mean(dn * normed, axis=-1, keepdims=True)
        )
        df = df.reshape(8, 8, C)
        dpad[...] = jnp.zeros((16, 16, C), F32)
        for q in range(7):
            rows = [None] * 14
            for r in range(7):
                term = df * pk[b, 7 * r + q : 7 * r + q + 1, :]
                for i in range(8):
                    part = term[i]
                    rows[r + i] = part if rows[r + i] is None else rows[r + i] + part
            dpad[0:14, q : q + 8, :] += jnp.stack(rows)
        send_b[b] = dot(pt_m[...], dpad[...].reshape(256, C).astype(BF16)).astype(BF16)
        exchange(send_b.at[b], recv_b.at[b], bs_sem.at[b], br_sem.at[b], -1)

        small_out[b, 49:50, :] = jnp.sum(d_unit * normed, axis=0, keepdims=True)
        small_out[b, 50:51, :] = jnp.sum(up * mixed_s[b], axis=0, keepdims=True)
        small_out[b, 51:56, :] = jnp.zeros((5, C), F32)
        for q in range(7):
            cols = pad[b, 0:14, q : q + 8, :]
            for r in range(7):
                tap = 7 * r + q
                prod = jnp.sum(df * cols[r : r + 8], axis=0)
                small_out[b, tap : tap + 1, :] = jnp.sum(prod, axis=0, keepdims=True)
        whole_wait(pa.at[b], precv.at[0, b])
        whole_wait(pb.at[b], precv.at[1, b])

        @pl.when(seg == 0)
        def _():
            g = dot(
                jnp.concatenate([u_s[b], pa[b]], axis=0),
                jnp.concatenate([db_s[b], pb[b]], axis=0), 0, 0,
            )
            for j in range(8):
                g_out[b, 256 * j : 256 * j + 256, :] = g[:, 128 * j : 128 * j + 128].astype(BF16)

        @pl.when(seg == 1)
        def _():
            g = dot(
                jnp.concatenate([h_s[b], pb[b]], axis=0),
                jnp.concatenate([dm_s[b], pa[b]], axis=0), 0, 0,
            )
            for j in range(2):
                g_out[b, 1024 * j : 1024 * j + 1024, :] = g[:, 128 * j : 128 * j + 128].astype(BF16)

        whole_wait(recv_b.at[b], br_sem.at[b])
        back = dot(st_m[...], recv_b[b])
        up = (up + dpad[3:11, 3:11, :].reshape(64, C) + back).astype(BF16)
        if b == 0:
            dx_out[...] = up
        up = up.astype(F32)

    for copy in w_copies:
        copy.wait_send()
    for b in range(BLOCKS):
        whole_wait(send_f.at[b], fs_sem.at[b])
        whole_wait(send_b.at[b], bs_sem.at[b])

        @pl.when(seg == 0)
        def _():
            whole_wait(h_s.at[b], psend.at[0, b])
            whole_wait(dm_s.at[b], psend.at[1, b])

        @pl.when(seg == 1)
        def _():
            whole_wait(u_s.at[b], psend.at[0, b])
            whole_wait(db_s.at[b], psend.at[1, b])


def local(
    inputs, cotangent, side_owner, side_from, corner_from, corner_live,
    depth_kernel, norm_gain, in_weight, out_weight, layer_scale,
):
    n = lax.axis_size("tile")
    factor = (2 * n * 64) ** (-0.5)
    vmem = pl.BlockSpec(memory_space=pltpu.VMEM)
    smem = pl.BlockSpec(memory_space=pltpu.SMEM)
    hbm = pl.BlockSpec(memory_space=pl.ANY)
    V = pltpu.VMEM
    dma = pltpu.SemaphoreType.DMA
    dx, g, small = pl.pallas_call(
        functools.partial(kernel, n),
        out_shape=(
            jax.ShapeDtypeStruct((64, C), BF16),
            jax.ShapeDtypeStruct((BLOCKS, 2048, 128), BF16),
            jax.ShapeDtypeStruct((BLOCKS, SMALL, C), F32),
        ),
        in_specs=[vmem, vmem, smem, smem, smem, smem, vmem, vmem, vmem, hbm, hbm],
        out_specs=(vmem, vmem, vmem),
        scratch_shapes=[
            V((BLOCKS, C, HID), BF16), V((BLOCKS, HID, C), BF16), V((BLOCKS, SMALL, C), F32),
            V((256, 64), BF16), V((64, 256), BF16), V((256, 256), BF16), V((256, 256), BF16),
            V((BLOCKS, 16, 16, C), F32), V((16, 16, C), F32),
            V((BLOCKS, 64, C), F32), V((BLOCKS, 64, 128), F32), V((BLOCKS, 64, C), F32),
            V((64, HID), F32), V((BLOCKS, 64, HID), F32),
            V((BLOCKS, 64, C), BF16), V((BLOCKS, 64, HID), BF16),
            V((BLOCKS, 64, C), BF16), V((BLOCKS, 64, HID), BF16),
            V((BLOCKS, 64, C), BF16), V((BLOCKS, 64, HID), BF16),
            V((BLOCKS, 256, C), BF16), V((BLOCKS, 256, C), BF16),
            V((BLOCKS, 256, C), BF16), V((BLOCKS, 256, C), BF16),
            dma((2, BLOCKS)), dma((2, 2)), dma((2,)),
            dma((BLOCKS,)), dma((BLOCKS,)), dma((BLOCKS,)), dma((BLOCKS,)),
            dma((2, BLOCKS)), dma((2, BLOCKS)),
        ],
        compiler_params=pltpu.CompilerParams(
            collective_id=0, has_side_effects=True, vmem_limit_bytes=40 * 1024 * 1024
        ),
    )(
        inputs.reshape(2, 64, C), cotangent.reshape(2, 64, C),
        side_owner, side_from, corner_from, corner_live,
        depth_kernel, norm_gain, layer_scale, in_weight, out_weight,
    )
    g = lax.psum(g, "tile")
    g = lax.all_to_all(g.reshape(2, 2, 2048, 128), "segment", 0, 0)
    g = g.astype(F32) * factor
    small = lax.psum(small, ("segment", "tile")) * factor
    small = lax.dynamic_slice_in_dim(small, 2 * lax.axis_index("segment"), 2, 0)
    d_in = g[0].reshape(2, 8, 256, 128).transpose(0, 2, 1, 3).reshape(2, C, HID)
    d_out = g[1].reshape(2, 2, 1024, 128).transpose(0, 2, 1, 3).reshape(2, HID, C)
    return dx.reshape(1, 8, 8, C), small[:, 0:49], small[:, 49], d_in, d_out, small[:, 50]


def solution(mesh):
    in_specs = (
        P(None, "tile", None, None), P(None, "tile", None, None),
        P(), P(), P(), P(),
        P("segment", None, None), P("segment", None), P("segment", None, None),
        P("segment", None, None), P("segment", None),
    )
    out_specs = (
        P("segment", "tile", None, None), P("segment", None, None), P("segment", None),
        P("segment", None, None), P("segment", None, None), P("segment", None),
    )
    return jax.shard_map(local, mesh=mesh, in_specs=in_specs, out_specs=out_specs, check_vma=False)
```

profile of v0, /device:TPU:4, one launch (start us, length us, event | category | flops | bytes accessed | tf_op | source)
XLA Modules:
  0.0 591.5 jit_solution(14209127264580537017)
XLA Ops:
  7.2 0.0 all-reduce.3.cloned.1.call-start
  7.2 0.8 copy.21.dk
  8.0 0.8 copy.17.so
  8.8 0.8 copy.18.sf
  9.6 0.8 copy.19.cf
  10.4 0.8 copy.20.cl
  11.2 0.0 copy-start
  11.2 1.2 copy-done
  12.4 0.0 copy-start.1
  12.4 1.2 copy-done.1
  13.6 0.0 copy-start.2
  13.6 0.8 copy-done.2
  14.5 0.0 copy-start.3
  14.5 0.8 copy-done.3
  15.3 0.0 copy-start.4
  15.3 0.7 copy-done.4
  16.0 0.0 copy-start.5
  16.0 0.7 copy-done.5
  16.7 69.8 %shard_map.154 = (bf16[64,256]{1,0:T(8,128)(2,1)S(1)}, bf16[4,2048,128]{2,1,0:T(8,128)(2,1)}, f32[4,56,256]{2,1,0:T(8,128)}) custom-call(bf16[2,64,256]{2,1,0:T(8,128)(2,1)S(1)} %bitcast.19, bf16[2,64,256]{2,1,0:T(8,128)(2,1)S(1)} %bitcast.20, s32[128,4]{1,0:T(8,128)S(1)} %copy.17.so, s32[128,4]{1,0:T(8,128)S(1)} %copy.18.sf, s32[128,4]{1,0:T(8,128)S(1)} %copy.19.cf, ...), custom_call_target="tpu_custom_call" | custom-call | tf_op jit(solution)/shard_map/pallas_call | solution.py:362
  86.5 0.0 all-reduce.3.cloned.1.call-update
  86.5 0.0 all-reduce.5.cloned.1.call-start
  86.6 0.7 all-reduce.5.cloned.1.call-update
  87.3 249.8 %all-reduce.3.cloned.1.call-done = f32[4,56,256]{2,1,0:T(8,128)} async-done(((f32[4,56,256]{2,1,0:T(8,128)}), f32[4,56,256]{2,1,0:T(8,128)}) %all-reduce.3.cloned.1.call-update) | async-done | bytes 229392 | tf_op jit(solution)/shard_map/psum | solution.py:397
  337.1 0.9 dynamic-slice_multiply_fusion
  338.0 0.7 copy.24
  338.7 0.6 copy_bitcast_fusion.2
  339.3 227.6 %all-reduce.5.cloned.1.call-done = bf16[2,2,2048,128]{3,2,1,0:T(8,128)(2,1)} async-done(((bf16[2,2,2048,128]{3,2,1,0:T(8,128)(2,1)}), bf16[2,2,2048,128]{3,2,1,0:T(8,128)(2,1)}) %all-reduce.5.cloned.1.call-update) | async-done | bytes 2097168 | tf_op jit(solution)/shard_map/psum | solution.py:394
  567.0 6.6 %all_to_all.5 = bf16[2,2,2048,128]{3,2,1,0:T(8,128)(2,1)S(1)} all-to-all(bf16[2,2,2048,128]{3,2,1,0:T(8,128)(2,1)} %all-reduce.5.cloned.1.call-done), channel_id=1, replica_groups=mesh['segment'=2,'tile'=128] {'segment'}, dimensions={0} | all-to-all | bytes 4194304 | tf_op jit(solution)/shard_map/all_to_all | solution.py:395
  573.6 0.3 convert_multiply_fusion
  573.9 1.6 fusion
  575.5 1.6 copy.31
  577.1 2.7 reshape.35
  579.8 2.8 copy.32
  582.6 1.5 reshape.34
  584.1 0.6 copy.36
  (1 shorter events, 0.0 us)
Async XLA Ops:
  7.2 330.0 %all-reduce.3.cloned.1.call-start = ((), (), s32[]{:S(2)}) async-start(), calls=%async_computation.1 | async-start | bytes 458752 | tf_op jit(solution)/shard_map/psum | solution.py:397
  11.2 1.2 copy-start
  12.4 1.2 copy-start.1
  13.6 0.8 copy-start.2
  14.5 0.8 copy-start.3
  15.3 0.7 copy-start.4
  16.0 0.7 copy-start.5
  86.5 480.4 %all-reduce.5.cloned.1.call-start = ((), (), s32[]{:S(2)}) async-start(), calls=%async_computation.2 | async-start | bytes 4194304 | tf_op jit(solution)/shard_map/psum | solution.py:394
Sparse Core Ops, SparseCore 0:
  86.7 250.4 all-reduce.2
  342.6 224.3 all-reduce.4
where the time goes:
time: 593 us; the launch traced here: 592 us
  waiting for transfers between devices  478 us (81%)
  Pallas kernels  69.8 us (12%)
  local copies, waits for them, and re-layouts  21.5 us (4%)
  between operations  14.1 us (2%)
  blocking collectives  6.61 us (1%)
    psum x1, waiting for transfers between devices, local(): small = lax.psum(small, ('segment', 'tile')) * factor  250 us
    psum x1, waiting for transfers between devices, local(): g = lax.psum(g, 'tile')  228 us
    pallas_call x1, Pallas kernels, local(): pl.pallas_call(functools.partial(kernel, n), out_shape=(jax.ShapeDtypeStr...  69.8 us
  transfers between devices with their start and end apart: 2, of which 2 were waited for; matrix products, arithmetic and copies ran while one was open for 0% of the time, Pallas kernels for 0%

commit v1 on v0

--- a/solution.py
+++ b/solution.py
@@ -22,7 +22,9 @@
 ROWS = (32, 32, 16, 32, 32, 16, 16, 32, 32, 16)
 BASE = (0, 32, 192, 64, 96, 208, 224, 128, 160, 240)
 SEND_ORDER = (2, 5, 6, 9, 3, 4, 7, 8, 0, 1)
-SMALL = 56
+SMALL = 64
+NX, NY, NZ = 4, 4, 8
+VMEM_BYTES = 60 * 1024 * 1024
 
 
 def dot(a, b, da=1, db=0):
@@ -37,32 +39,32 @@
 
 
 def seam_steps(so, t, n):
-    north = lax.rem(so[t, 0] - t + GW + n, n)
-    south = lax.rem(t + GW - so[t, 2] + n, n)
+    north = lax.rem(so[0, t] - t + GW + n, n)
+    south = lax.rem(t + GW - so[2, t] + n, n)
     return north, south
 
 
 def wanted_rim(slot, t, so, sf, cf, n):
     north, south = seam_steps(so, t, n)
     if slot == 0:
-        return sf[t, 3]
+        return sf[3, t]
     if slot == 1:
-        return sf[t, 1]
+        return sf[1, t]
     if slot == 2:
-        return cf[t, 0]
+        return cf[0, t]
     if slot == 3:
-        return jnp.where(north == 0, sf[t, 0], cf[t, 0])
+        return jnp.where(north == 0, sf[0, t], cf[0, t])
     if slot == 4:
-        return jnp.where(north == 1, sf[t, 0], cf[t, 1])
+        return jnp.where(north == 1, sf[0, t], cf[1, t])
     if slot == 5:
-        return cf[t, 1]
+        return cf[1, t]
     if slot == 6:
-        return cf[t, 2]
+        return cf[2, t]
     if slot == 7:
-        return jnp.where(south == 0, sf[t, 2], cf[t, 2])
+        return jnp.where(south == 0, sf[2, t], cf[2, t])
     if slot == 8:
-        return jnp.where(south == 1, sf[t, 2], cf[t, 3])
-    return cf[t, 3]
+        return jnp.where(south == 1, sf[2, t], cf[3, t])
+    return cf[3, t]
 
 
 def send_matrix(me, n, so, sf, cf):
@@ -101,7 +103,7 @@
 
     x = lax.broadcasted_iota(jnp.int32, (16, 256), 0)
     lane = lax.broadcasted_iota(jnp.int32, (16, 256), 1)
-    live = [cl[me, c] == 1 for c in range(4)]
+    live = [cl[c, me] == 1 for c in range(4)]
 
     def corner(c, i, j):
         zero, sa, sb = ((nz, 2, 3), (nz, 4, 5), (sz, 6, 7), (sz, 8, 9))[c]
@@ -134,54 +136,139 @@
 
 def kernel(
     n,
-    xin, cot, so, sf, cf, cl, dk, ng, ls, win_in, wout_in,
-    dx_out, g_out, small_out,
+    xin, cot, so_in, sf_in, cf_in, cl_in, dk_in, ng_in, ls_in, win_in, wout_in,
+    dx_out, gin_out, gout_out, small_s,
+    g_s, r1, g2, r2, g3, r3, ag, sm, sr0, s0, sr1, s1, sr2, s2, sr3, s3,
+    so, sf, cf, cl, x_s, x0_s, cot_s, s0_m, dk_s, ng_s, ls_s,
     win, wout, pk, s_m, st_m, p_m, pt_m,
     pad, dpad, normed_s, inv_s, mixed_s, before_s, slope_s,
     u_s, h_s, dm_s, db_s, pa, pb,
     send_f, recv_f, send_b, recv_b,
     wsem, wsend, pksem, fs_sem, fr_sem, bs_sem, br_sem, psend, precv,
+    ms_sem, mr_sem, go_sem, ss_sem, sr_sem, so_sem, in_sem, xr_sem,
 ):
     seg = lax.axis_index("segment")
     me = lax.axis_index("tile")
     other = 1 - seg
 
+    seams = [
+        pltpu.make_async_copy(src, dst, in_sem.at[k])
+        for k, (src, dst) in enumerate(((so_in, so), (sf_in, sf), (cf_in, cf), (cl_in, cl)))
+    ]
+    x_copy = pltpu.make_async_copy(xin.at[seg], x_s, in_sem.at[4])
+    small_in = [
+        pltpu.make_async_copy(src, dst, in_sem.at[5 + k])
+        for k, (src, dst) in enumerate(((dk_in, dk_s), (ng_in, ng_s), (ls_in, ls_s)))
+    ]
+    for copy in [*seams, x_copy, *small_in]:
+        copy.start()
+
+    z = lax.rem(me, NZ)
+    y = lax.rem(me // NZ, NY)
+    x = me // (NZ * NY)
+    at1, at2 = x + seg * (y - x), y + seg * (x - y)
+    stride1 = NY * NZ - seg * (NY * NZ - NZ)
+    stride2 = NZ + seg * (NY * NZ - NZ)
+
+    def device_of(t):
+        row = t // NZ
+        hi = row // NY
+        lo = row - hi * NY
+        lo = lo + lax.rem(hi, 2) * (NY - 1 - 2 * lo)
+        return (hi * NY + lo) * NZ + lax.rem(t, NZ)
+
+    odd = lax.rem(x, 2)
+    tile = device_of(me)
+    mirror = tile
+
+    def peer1(d):
+        to = lax.rem(at1 + d, NX)
+        return to, me + (to - at1) * stride1
+
+    def peer2(d):
+        to = lax.rem(at2 + d, NX)
+        return to, me + (to - at2) * stride2
+
+    def peer3(d):
+        to = lax.rem(z + d, NZ)
+        return to, me + to - z
+
+    barrier = pltpu.get_barrier_semaphore()
+    partners = [(seg, peer1(d)[1]) for d in range(1, NX)]
+    partners += [(other, peer1(d)[1]) for d in range(1, NX)]
+    partners += [(seg, peer2(d)[1]) for d in range(1, NX)]
+    partners += [(other, peer2(d)[1]) for d in range(1, NX)]
+    partners += [(seg, peer3(d)[1]) for d in range(1, NZ)]
+    for off in OFFSETS:
+        if abs(off) != GW:
+            partners.append((seg, lax.rem(tile + off + n, n)))
+        partners.append((seg, device_of(lax.rem(tile + off + n, n))))
+    partners.append((other, me))
+    for partner in partners:
+        pl.semaphore_signal(barrier, inc=1, device_id=partner, device_id_type=MESH)
+
+    @pl.when(odd == 1)
+    def _():
+        pl.semaphore_signal(barrier, inc=1, device_id=(seg, mirror), device_id_type=MESH)
+
+    stays = {off: tile == lax.rem(me - off + n, n) for off in (-GW, GW)}
+    signals = len(partners) + odd
+    for off, stay in stays.items():
+        signals = signals + jnp.where(stay, 0, 1)
+
+        @pl.when(jnp.logical_not(stay))
+        def _():
+            pl.semaphore_signal(
+                barrier, inc=1, device_id=(seg, lax.rem(tile + off + n, n)), device_id_type=MESH
+            )
+
+    mine = pl.ds(2 * seg, 2)
     for l in range(2):
         b = 2 * seg + l
         pltpu.make_async_copy(win_in.at[l], win.at[b], wsem.at[0, b]).start()
         pltpu.make_async_copy(wout_in.at[l], wout.at[b], wsem.at[1, b]).start()
 
-    barrier = pltpu.get_barrier_semaphore()
-    for off in OFFSETS:
-        pl.semaphore_signal(
-            barrier, inc=1, device_id=(seg, lax.rem(me - off + n, n)), device_id_type=MESH
-        )
-    pl.semaphore_signal(barrier, inc=1, device_id=(other, me), device_id_type=MESH)
-
+    for copy in seams:
+        copy.wait()
+    s0_m[...] = send_matrix(me, n, so, sf, cf).astype(BF16)
+    x_copy.wait()
+    send_f[0] = dot(s0_m[...], x_s[...]).astype(BF16)
+
+    for copy in small_in:
+        copy.wait()
+    taps = dk_s[...].astype(F32)
     for l in range(2):
         b = 2 * seg + l
-        pk[b, 0:49, :] = dk[l].astype(F32)
-        pk[b, 49:50, :] = ng[l : l + 1, :]
-        pk[b, 50:51, :] = ls[l : l + 1, :]
-        pk[b, 51:56, :] = jnp.zeros((5, C), F32)
-    s_f = send_matrix(me, n, so, sf, cf)
-    s_m[...] = s_f.astype(BF16)
-    curb = xin[seg]
-    send_f[0] = dot(s_m[...], curb).astype(BF16)
-
-    pl.semaphore_wait(barrier, len(OFFSETS) + 1)
-
-    def exchange(src, dst, ssem, rsem, sign):
+        pk[b, 0:49, :] = taps[:, l, :]
+        pk[b, 49:50, :] = ng_s[l : l + 1, :]
+        pk[b, 50:51, :] = ls_s[l : l + 1, :]
+        pk[b, 51:64, :] = jnp.zeros((13, C), F32)
+
+    pl.semaphore_wait(barrier, signals)
+
+    def exchange(src, dst, ssem, rsem, sign, home):
         for slot in SEND_ORDER:
+            off = OFFSETS[slot]
             rows = pl.ds(BASE[slot], ROWS[slot])
-            pltpu.make_async_remote_copy(
-                src_ref=src.at[rows],
-                dst_ref=dst.at[rows],
-                send_sem=ssem,
-                recv_sem=rsem,
-                device_id=(seg, lax.rem(me - sign * OFFSETS[slot] + n, n)),
-                device_id_type=MESH,
-            ).start()
+
+            def go():
+                pltpu.make_async_remote_copy(
+                    src_ref=src.at[rows],
+                    dst_ref=dst.at[rows],
+                    send_sem=ssem,
+                    recv_sem=rsem,
+                    device_id=(seg, device_of(lax.rem(home - sign * off + n, n))),
+                    device_id_type=MESH,
+                ).start()
+
+            if home is tile or off not in stays:
+                go()
+            else:
+                pl.when(jnp.logical_not(stays[off]))(go)
+
+                @pl.when(stays[off])
+                def _():
+                    pltpu.make_async_copy(src.at[rows], dst.at[rows], rsem).start()
 
     def to_partner(src, dst, ssem, rsem):
         return pltpu.make_async_remote_copy(
@@ -189,8 +276,21 @@
             device_id=(other, me), device_id_type=MESH,
         )
 
-    exchange(send_f.at[0], recv_f.at[0], fs_sem.at[0], fr_sem.at[0], 1)
-    mine = pl.ds(2 * seg, 2)
+    exchange(send_f.at[0], recv_f.at[0], fs_sem.at[0], fr_sem.at[0], 1, me)
+
+    @pl.when(odd == 1)
+    def _():
+        for k, (src, dst) in enumerate(((xin, x0_s), (cot, cot_s))):
+            pltpu.make_async_remote_copy(
+                src_ref=src.at[seg], dst_ref=dst, send_sem=xr_sem.at[0, k], recv_sem=xr_sem.at[1, k],
+                device_id=(seg, mirror), device_id_type=MESH,
+            ).start()
+
+    @pl.when(odd == 0)
+    def _():
+        for k, (src, dst) in enumerate(((xin, x0_s), (cot, cot_s))):
+            pltpu.make_async_copy(src.at[seg], dst, xr_sem.at[1, k]).start()
+
     pk_copy = to_partner(pk.at[mine], pk.at[mine], pksem.at[0], pksem.at[1])
     pk_copy.start()
     w_copies = []
@@ -201,11 +301,131 @@
     for copy in w_copies:
         copy.start()
 
+    s_f = send_matrix(tile, n, so, sf, cf)
+    s_m[...] = s_f.astype(BF16)
     st_m[...] = jnp.transpose(s_f).astype(BF16)
-    p_f = place_matrix(me, n, so, cl)
+    p_f = place_matrix(tile, n, so, cl)
     p_m[...] = p_f.astype(BF16)
     pt_m[...] = jnp.transpose(p_f).astype(BF16)
     pk_copy.wait()
+    whole_wait(x0_s, xr_sem.at[1, 0])
+    curb = x0_s[...]
+
+    q1, q2, q3 = 2048 // NX, 2048 // NX // NX, 2048 // NX // NX // NZ
+    w1 = 64 // NX
+
+    def send(src, dst, ssem, rsem, device):
+        pltpu.make_async_remote_copy(
+            src_ref=src, dst_ref=dst, send_sem=ssem, recv_sem=rsem,
+            device_id=device, device_id_type=MESH,
+        ).start()
+
+    def main_chain(b):
+        l, owner = b % 2, b // 2
+        for d in range(1, NX):
+            to, t = peer1(d)
+            send(g_s.at[b, pl.ds(to * q1, q1)], r1.at[b, d - 1], ms_sem.at[0, b], mr_sem.at[0, b], (seg, t))
+        yield
+        whole_wait(r1.at[b], mr_sem.at[0, b])
+        total = g_s[b, pl.ds(at1 * q1, q1), :].astype(F32)
+        for d in range(NX - 1):
+            total = total + r1[b, d].astype(F32)
+        g2[b] = total.astype(BF16)
+        for d in range(1, NX):
+            to, t = peer2(d)
+            send(g2.at[b, pl.ds(to * q2, q2)], r2.at[b, d - 1], ms_sem.at[1, b], mr_sem.at[1, b], (seg, t))
+        yield
+        whole_wait(r2.at[b], mr_sem.at[1, b])
+        total = g2[b, pl.ds(at2 * q2, q2), :].astype(F32)
+        for d in range(NX - 1):
+            total = total + r2[b, d].astype(F32)
+        g3[b] = total.astype(BF16)
+        for d in range(1, NZ):
+            to, t = peer3(d)
+            send(g3.at[b, pl.ds(to * q3, q3)], r3.at[b, d - 1], ms_sem.at[2, b], mr_sem.at[2, b], (seg, t))
+        yield
+        whole_wait(r3.at[b], mr_sem.at[2, b])
+        total = g3[b, pl.ds(z * q3, q3), :].astype(F32)
+        for d in range(NZ - 1):
+            total = total + r3[b, d].astype(F32)
+        here = pl.ds(at2 * q2 + z * q3, q3)
+        ag[b, here, :] = total.astype(BF16)
+        for d in range(1, NZ):
+            send(ag.at[b, here], ag.at[b, here], ms_sem.at[3, b], mr_sem.at[3, b], (seg, peer3(d)[1]))
+        yield
+        whole_wait(ag.at[b, pl.ds(0, (NZ - 1) * q3)], mr_sem.at[3, b])
+        here2 = pl.ds(at2 * q2, q2)
+        for d in range(1, NX):
+            send(ag.at[b, here2], ag.at[b, here2], ms_sem.at[4, b], mr_sem.at[4, b], (seg, peer2(d)[1]))
+        yield
+        whole_wait(ag.at[b, pl.ds(0, (NX - 1) * q2)], mr_sem.at[4, b])
+        for kind in range(2):
+
+            @pl.when(seg == kind)
+            def _():
+                if kind == 0:
+                    first = pl.multiple_of(at1 * (q1 // 2), 128)
+                    pairs = [
+                        (ag.at[b, pl.ds(256 * j, 256)], gin_out.at[l, :, pl.ds(first + 128 * j, 128)])
+                        for j in range(q1 // 256)
+                    ]
+                else:
+                    rows = pl.multiple_of(lax.rem(at1 * q1, 1024), 16)
+                    column = pl.multiple_of((at1 * q1 // 1024) * 128, 128)
+                    pairs = [(ag.at[b], gout_out.at[l, pl.ds(rows, q1), pl.ds(column, 128)])]
+                for d in range(1, NX):
+                    for src, dst in pairs:
+                        send(src, dst, ms_sem.at[5, b], go_sem.at[l, kind], (owner, peer1(d)[1]))
+                for src, dst in pairs:
+                    if kind == owner:
+                        pltpu.make_async_copy(src, dst, go_sem.at[l, kind]).start()
+                    else:
+                        send(src, dst, ms_sem.at[6, b], go_sem.at[l, kind], (other, me))
+
+    def small_chain(b):
+        l, owner = b % 2, b // 2
+        send(sm.at[b, pl.ds(other * 64, 64)], sr0.at[b], ss_sem.at[0, b], sr_sem.at[0, b], (other, me))
+        yield
+        whole_wait(sr0.at[b], sr_sem.at[0, b])
+        s0[b] = sm[b, pl.ds(seg * 64, 64), :] + sr0[b]
+        for d in range(1, NX):
+            to, t = peer1(d)
+            send(s0.at[b, pl.ds(to * w1, w1)], sr1.at[b, d - 1], ss_sem.at[1, b], sr_sem.at[1, b], (seg, t))
+        yield
+        whole_wait(sr1.at[b], sr_sem.at[1, b])
+        s1[b] = s0[b, pl.ds(at1 * w1, w1), :] + jnp.sum(sr1[b], axis=0)
+        for d in range(1, NX):
+            send(s1.at[b], sr2.at[b, d - 1], ss_sem.at[2, b], sr_sem.at[2, b], (seg, peer2(d)[1]))
+        yield
+        whole_wait(sr2.at[b], sr_sem.at[2, b])
+        s2[b] = s1[b] + jnp.sum(sr2[b], axis=0)
+        for d in range(1, NZ):
+            send(s2.at[b], sr3.at[b, d - 1], ss_sem.at[3, b], sr_sem.at[3, b], (seg, peer3(d)[1]))
+        yield
+        whole_wait(sr3.at[b], sr_sem.at[3, b])
+        s3[b] = s2[b] + jnp.sum(sr3[b], axis=0)
+        out = small_s.at[l, pl.ds(seg * 64 + at1 * w1, w1)]
+        for d in range(1, NX):
+            send(s3.at[b], out, ss_sem.at[4, b], so_sem.at[l], (owner, peer1(d)[1]))
+
+        @pl.when(seg == owner)
+        def _():
+            pltpu.make_async_copy(s3.at[b], out, so_sem.at[l]).start()
+
+        @pl.when(seg != owner)
+        def _():
+            send(s3.at[b], out, ss_sem.at[5, b], so_sem.at[l], (other, me))
+
+    chains = []
+
+    def begin(chain):
+        next(chain)
+        chains.append(chain)
+
+    def advance(which=None):
+        for chain in list(chains if which is None else which):
+            if chain in chains and next(chain, True):
+                chains.remove(chain)
 
     def slope_of(b):
         before = before_s[...]
@@ -217,7 +437,7 @@
     for b in range(BLOCKS):
         if b > 0:
             send_f[b] = dot(s_m[...], curb).astype(BF16)
-            exchange(send_f.at[b], recv_f.at[b], fs_sem.at[b], fr_sem.at[b], 1)
+            exchange(send_f.at[b], recv_f.at[b], fs_sem.at[b], fr_sem.at[b], 1, tile)
             slope_of(b - 1)
         cur = curb.astype(F32)
         whole_wait(recv_f.at[b], fr_sem.at[b])
@@ -254,7 +474,8 @@
         def _():
             to_partner(u_s.at[b], pa.at[b], psend.at[0, b], precv.at[0, b]).start()
 
-    up = cot[seg].astype(F32)
+    whole_wait(cot_s, xr_sem.at[1, 1])
+    up = cot_s[...].astype(F32)
     slope_of(BLOCKS - 1)
     for b in reversed(range(BLOCKS)):
         dm = (up * pk[b, 50:51, :]).astype(BF16)
@@ -282,6 +503,53 @@
             - normed * jnp.mean(dn * normed, axis=-1, keepdims=True)
         )
         df = df.reshape(8, 8, C)
+        older = list(chains)
+
+        def put(row, value):
+            sm[b, row : row + 1, :] = value[:, 0:128]
+            sm[b, 64 + row : 65 + row, :] = value[:, 128:256]
+
+        def small_grads():
+            put(49, jnp.sum(d_unit * normed, axis=0, keepdims=True))
+            put(50, jnp.sum(up * mixed_s[b], axis=0, keepdims=True))
+            sm[b, 51:64, :] = jnp.zeros((13, 128), F32)
+            sm[b, 115:128, :] = jnp.zeros((13, 128), F32)
+            for q in range(7):
+                cols = pad[b, 0:14, q : q + 8, :]
+                for r in range(7):
+                    tap = 7 * r + q
+                    prod = jnp.sum(df * cols[r : r + 8], axis=0)
+                    put(tap, jnp.sum(prod, axis=0, keepdims=True))
+            begin(small_chain(b))
+
+        def weight_grads():
+            whole_wait(pa.at[b], precv.at[0, b])
+            whole_wait(pb.at[b], precv.at[1, b])
+
+            @pl.when(seg == 0)
+            def _():
+                g = dot(
+                    jnp.concatenate([u_s[b], pa[b]], axis=0),
+                    jnp.concatenate([db_s[b], pb[b]], axis=0), 0, 0,
+                )
+                for j in range(8):
+                    g_s[b, 256 * j : 256 * j + 256, :] = g[:, 128 * j : 128 * j + 128].astype(BF16)
+
+            @pl.when(seg == 1)
+            def _():
+                g = dot(
+                    jnp.concatenate([h_s[b], pb[b]], axis=0),
+                    jnp.concatenate([dm_s[b], pa[b]], axis=0), 0, 0,
+                )
+                for j in range(2):
+                    g_s[b, 1024 * j : 1024 * j + 1024, :] = g[:, 128 * j : 128 * j + 128].astype(BF16)
+
+            begin(main_chain(b))
+
+        if b == 0:
+            weight_grads()
+            small_grads()
+        advance(older)
         dpad[...] = jnp.zeros((16, 16, C), F32)
         for q in range(7):
             rows = [None] * 14
@@ -292,50 +560,75 @@
                     rows[r + i] = part if rows[r + i] is None else rows[r + i] + part
             dpad[0:14, q : q + 8, :] += jnp.stack(rows)
         send_b[b] = dot(pt_m[...], dpad[...].reshape(256, C).astype(BF16)).astype(BF16)
-        exchange(send_b.at[b], recv_b.at[b], bs_sem.at[b], br_sem.at[b], -1)
-
-        small_out[b, 49:50, :] = jnp.sum(d_unit * normed, axis=0, keepdims=True)
-        small_out[b, 50:51, :] = jnp.sum(up * mixed_s[b], axis=0, keepdims=True)
-        small_out[b, 51:56, :] = jnp.zeros((5, C), F32)
-        for q in range(7):
-            cols = pad[b, 0:14, q : q + 8, :]
-            for r in range(7):
-                tap = 7 * r + q
-                prod = jnp.sum(df * cols[r : r + 8], axis=0)
-                small_out[b, tap : tap + 1, :] = jnp.sum(prod, axis=0, keepdims=True)
-        whole_wait(pa.at[b], precv.at[0, b])
-        whole_wait(pb.at[b], precv.at[1, b])
-
-        @pl.when(seg == 0)
-        def _():
-            g = dot(
-                jnp.concatenate([u_s[b], pa[b]], axis=0),
-                jnp.concatenate([db_s[b], pb[b]], axis=0), 0, 0,
-            )
-            for j in range(8):
-                g_out[b, 256 * j : 256 * j + 256, :] = g[:, 128 * j : 128 * j + 128].astype(BF16)
-
-        @pl.when(seg == 1)
-        def _():
-            g = dot(
-                jnp.concatenate([h_s[b], pb[b]], axis=0),
-                jnp.concatenate([dm_s[b], pa[b]], axis=0), 0, 0,
-            )
-            for j in range(2):
-                g_out[b, 1024 * j : 1024 * j + 1024, :] = g[:, 128 * j : 128 * j + 128].astype(BF16)
-
+        exchange(send_b.at[b], recv_b.at[b], bs_sem.at[b], br_sem.at[b], -1, tile)
+
+        advance(older)
+        if b > 0:
+            small_grads()
+            weight_grads()
         whole_wait(recv_b.at[b], br_sem.at[b])
         back = dot(st_m[...], recv_b[b])
         up = (up + dpad[3:11, 3:11, :].reshape(64, C) + back).astype(BF16)
         if b == 0:
-            dx_out[...] = up
+            x_s[...] = up
+
+            @pl.when(odd == 1)
+            def _():
+                pltpu.make_async_remote_copy(
+                    src_ref=x_s, dst_ref=dx_out, send_sem=xr_sem.at[0, 2], recv_sem=xr_sem.at[1, 2],
+                    device_id=(seg, mirror), device_id_type=MESH,
+                ).start()
+
+            @pl.when(odd == 0)
+            def _():
+                pltpu.make_async_copy(x_s, dx_out, xr_sem.at[1, 2]).start()
+
         up = up.astype(F32)
+
+    while chains:
+        advance()
+    for l in range(2):
+        whole_wait(small_s.at[l], so_sem.at[l])
+        whole_wait(gin_out.at[l], go_sem.at[l, 0])
+        whole_wait(gout_out.at[l], go_sem.at[l, 1])
+    whole_wait(dx_out, xr_sem.at[1, 2])
+    stay = jnp.logical_or(stays[-GW], stays[GW])
+
+    @pl.when(stay)
+    def _():
+        whole_wait(send_f.at[0, pl.ds(0, 224)], fs_sem.at[0])
+
+    @pl.when(jnp.logical_not(stay))
+    def _():
+        whole_wait(send_f.at[0], fs_sem.at[0])
+
+    @pl.when(odd == 1)
+    def _():
+        for k in range(3):
+            whole_wait(x_s, xr_sem.at[0, k])
 
     for copy in w_copies:
         copy.wait_send()
     for b in range(BLOCKS):
-        whole_wait(send_f.at[b], fs_sem.at[b])
+        if b > 0:
+            whole_wait(send_f.at[b], fs_sem.at[b])
         whole_wait(send_b.at[b], bs_sem.at[b])
+        whole_wait(r1.at[b], ms_sem.at[0, b])
+        whole_wait(r2.at[b], ms_sem.at[1, b])
+        whole_wait(r3.at[b], ms_sem.at[2, b])
+        whole_wait(r3.at[b], ms_sem.at[3, b])
+        whole_wait(r2.at[b], ms_sem.at[4, b])
+        whole_wait(r1.at[b], ms_sem.at[5, b])
+        whole_wait(sr0.at[b], ss_sem.at[0, b])
+        whole_wait(sr1.at[b], ss_sem.at[1, b])
+        whole_wait(sr2.at[b], ss_sem.at[2, b])
+        whole_wait(sr3.at[b], ss_sem.at[3, b])
+        whole_wait(sr1.at[b], ss_sem.at[4, b])
+
+        @pl.when(seg != b // 2)
+        def _():
+            whole_wait(ag.at[b], ms_sem.at[6, b])
+            whole_wait(s3.at[b], ss_sem.at[5, b])
 
         @pl.when(seg == 0)
         def _():
@@ -346,6 +639,17 @@
         def _():
             whole_wait(u_s.at[b], psend.at[0, b])
             whole_wait(db_s.at[b], psend.at[1, b])
+
+
+def finish(factor, dx, gin, gout, small, dx_out, gin_out, gout_out, gk_out, gg_out, gs_out):
+    gin_out[...] = gin[...].astype(F32) * factor
+    gout_out[...] = gout[...].astype(F32) * factor
+    dx_out[...] = dx[...].reshape(dx_out.shape)
+    for l in range(2):
+        total = jnp.concatenate([small[l, 0:64, :], small[l, 64:128, :]], axis=1) * factor
+        gk_out[:, l, :] = total[0:49]
+        gg_out[l : l + 1, :] = total[49:50]
+        gs_out[l : l + 1, :] = total[50:51]
 
 
 def local(
@@ -355,20 +659,31 @@
     n = lax.axis_size("tile")
     factor = (2 * n * 64) ** (-0.5)
     vmem = pl.BlockSpec(memory_space=pltpu.VMEM)
-    smem = pl.BlockSpec(memory_space=pltpu.SMEM)
     hbm = pl.BlockSpec(memory_space=pl.ANY)
     V = pltpu.VMEM
+    S = pltpu.SMEM
+    shape = jax.ShapeDtypeStruct
+    q1, q2, q3 = 2048 // NX, 2048 // NX // NX, 2048 // NX // NX // NZ
+    w1 = 64 // NX
     dma = pltpu.SemaphoreType.DMA
-    dx, g, small = pl.pallas_call(
+    dx, d_in, d_out, small = pl.pallas_call(
         functools.partial(kernel, n),
         out_shape=(
-            jax.ShapeDtypeStruct((64, C), BF16),
-            jax.ShapeDtypeStruct((BLOCKS, 2048, 128), BF16),
-            jax.ShapeDtypeStruct((BLOCKS, SMALL, C), F32),
+            shape((64, C), BF16), shape((2, C, HID), BF16), shape((2, HID, C), BF16), shape((2, 128, 128), F32),
         ),
-        in_specs=[vmem, vmem, smem, smem, smem, smem, vmem, vmem, vmem, hbm, hbm],
-        out_specs=(vmem, vmem, vmem),
+        in_specs=[hbm] * 11,
+        out_specs=(hbm,) * 4,
         scratch_shapes=[
+            V((BLOCKS, 2048, 128), BF16), V((BLOCKS, NX - 1, q1, 128), BF16), V((BLOCKS, q1, 128), BF16),
+            V((BLOCKS, NX - 1, q2, 128), BF16), V((BLOCKS, q2, 128), BF16), V((BLOCKS, NZ - 1, q3, 128), BF16),
+            V((BLOCKS, q1, 128), BF16), V((BLOCKS, 128, 128), F32),
+            V((BLOCKS, 64, 128), F32), V((BLOCKS, 64, 128), F32),
+            V((BLOCKS, NX - 1, w1, 128), F32), V((BLOCKS, w1, 128), F32),
+            V((BLOCKS, NX - 1, w1, 128), F32), V((BLOCKS, w1, 128), F32),
+            V((BLOCKS, NZ - 1, w1, 128), F32), V((BLOCKS, w1, 128), F32),
+            S((4, n), jnp.int32), S((4, n), jnp.int32), S((4, n), jnp.int32), S((4, n), jnp.int32),
+            V((64, C), BF16), V((64, C), BF16), V((64, C), BF16), V((256, 64), BF16),
+            V((49, 2, C), BF16), V((2, C), F32), V((2, C), F32),
             V((BLOCKS, C, HID), BF16), V((BLOCKS, HID, C), BF16), V((BLOCKS, SMALL, C), F32),
             V((256, 64), BF16), V((64, 256), BF16), V((256, 256), BF16), V((256, 256), BF16),
             V((BLOCKS, 16, 16, C), F32), V((16, 16, C), F32),
@@ -382,23 +697,41 @@
             dma((2, BLOCKS)), dma((2, 2)), dma((2,)),
             dma((BLOCKS,)), dma((BLOCKS,)), dma((BLOCKS,)), dma((BLOCKS,)),
             dma((2, BLOCKS)), dma((2, BLOCKS)),
+            dma((7, BLOCKS)), dma((5, BLOCKS)), dma((2, 2)), dma((6, BLOCKS)), dma((4, BLOCKS)), dma((2,)),
+            dma((8,)), dma((2, 3)),
         ],
         compiler_params=pltpu.CompilerParams(
-            collective_id=0, has_side_effects=True, vmem_limit_bytes=40 * 1024 * 1024
+            collective_id=0, has_side_effects=True, vmem_limit_bytes=VMEM_BYTES
         ),
     )(
         inputs.reshape(2, 64, C), cotangent.reshape(2, 64, C),
-        side_owner, side_from, corner_from, corner_live,
-        depth_kernel, norm_gain, layer_scale, in_weight, out_weight,
+        side_owner.T, side_from.T, corner_from.T, corner_live.T,
+        depth_kernel.transpose(1, 0, 2), norm_gain, layer_scale, in_weight, out_weight,
     )
-    g = lax.psum(g, "tile")
-    g = lax.all_to_all(g.reshape(2, 2, 2048, 128), "segment", 0, 0)
-    g = g.astype(F32) * factor
-    small = lax.psum(small, ("segment", "tile")) * factor
-    small = lax.dynamic_slice_in_dim(small, 2 * lax.axis_index("segment"), 2, 0)
-    d_in = g[0].reshape(2, 8, 256, 128).transpose(0, 2, 1, 3).reshape(2, C, HID)
-    d_out = g[1].reshape(2, 2, 1024, 128).transpose(0, 2, 1, 3).reshape(2, HID, C)
-    return dx.reshape(1, 8, 8, C), small[:, 0:49], small[:, 49], d_in, d_out, small[:, 50]
+    dx, d_in, d_out, d_kernel, d_gain, d_scale = pl.pallas_call(
+        functools.partial(finish, factor),
+        grid=(4,),
+        out_shape=(
+            shape((1, 8, 8, C), BF16), shape((2, C, HID), F32), shape((2, HID, C), F32),
+            shape((49, 2, C), F32), shape((2, C), F32), shape((2, C), F32),
+        ),
+        in_specs=[
+            pl.BlockSpec((64, C), lambda i: (0, 0)),
+            pl.BlockSpec((2, C // 4, HID), lambda i: (0, i, 0)),
+            pl.BlockSpec((2, HID // 4, C), lambda i: (0, i, 0)),
+            pl.BlockSpec((2, 128, 128), lambda i: (0, 0, 0)),
+        ],
+        out_specs=(
+            pl.BlockSpec((1, 8, 8, C), lambda i: (0, 0, 0, 0)),
+            pl.BlockSpec((2, C // 4, HID), lambda i: (0, i, 0)),
+            pl.BlockSpec((2, HID // 4, C), lambda i: (0, i, 0)),
+            pl.BlockSpec((49, 2, C), lambda i: (0, 0, 0)),
+            pl.BlockSpec((2, C), lambda i: (0, 0)),
+            pl.BlockSpec((2, C), lambda i: (0, 0)),
+        ),
+        compiler_params=pltpu.CompilerParams(vmem_limit_bytes=VMEM_BYTES),
+    )(dx, d_in, d_out, small)
+    return dx, d_kernel.transpose(1, 0, 2), d_gain, d_in, d_out, d_scale
 
 
 def solution(mesh):

time: 593 us -> 111 us (0.19)
  waiting for transfers between devices: 478 us -> 0 us
  Pallas kernels: 69.8 us -> 110 us
  local copies, waits for them, and re-layouts: 21.5 us -> 0 us
  between operations: 14.1 us -> 0.8 us
  blocking collectives: 6.61 us -> 0 us
    psum x2 -> x0, waiting for transfers between devices: 477 us -> none  [the longest x1 250 us: local(): small = lax.psum(small, ('segment', 'tile')) * factor]
    pallas_call x1 -> x2, Pallas kernels: 69.8 us -> 110 us  [the longest x1 105 us: local(): pl.pallas_call(functools.partial(kernel, n), out_shape=(shape((64, C), BF...]
    unnamed x20 -> x0, local copies, waits for them, and re-layouts: 11.3 us -> none
    all_to_all x1 -> x0, blocking collectives: 6.61 us -> none  [local(): g = lax.all_to_all(g.reshape(2, 2, 2048, 128), 'segment', 0, 0)]
  transfers between devices with their start and end apart: 2 -> 0, of which waited for: 2 -> 0; matrix products, arithmetic and copies ran while one was open for 0% -> 0% of each run, Pallas kernels for 0% -> 0%
where the time goes in v1:
time: 111 us
  Pallas kernels  110 us (99%)
    pallas_call x1, Pallas kernels, local(): pl.pallas_call(functools.partial(kernel, n), out_shape=(shape((64, C), BF...  105 us
    pallas_call x1, Pallas kernels, local(): pl.pallas_call(functools.partial(finish, factor), grid=(4,), out_shape=(s...  4.36 us

profile of v1, /device:TPU:4, one launch (start us, length us, event | category | flops | bytes accessed | tf_op | source)
XLA Modules:
  0.0 110.5 jit_solution(9501255829433326951)
XLA Ops:
  0.6 105.4 %shard_map.154 = (bf16[64,256]{1,0:T(8,128)(2,1)}, bf16[2,256,1024]{2,1,0:T(8,128)(2,1)}, bf16[2,1024,256]{2,1,0:T(8,128)(2,1)}, f32[2,128,128]{2,1,0:T(8,128)}) custom-call(bf16[2,64,256]{2,1,0:T(8,128)(2,1)} %bitcast.8, bf16[2,64,256]{2,1,0:T(8,128)(2,1)} %bitcast.9, s32[4,128]{1,0:T(4,128)} %bitcast.11, s32[4,128]{1,0:T(4,128)} %bitcast.12, ...), custom_call_target="tpu_custom_call" | custom-call | tf_op jit(solution)/shard_map/pallas_call | solution.py:669
  106.0 4.4 %shard_map.155 = (bf16[1,8,8,256]{3,2,1,0:T(8,128)(2,1)}, f32[2,256,1024]{2,1,0:T(8,128)}, f32[2,1024,256]{2,1,0:T(8,128)}, f32[49,2,256]{2,1,0:T(2,128)}, f32[2,256]{1,0:T(2,128)}, /*index=5*/f32[2,256]{1,0:T(2,128)}) custom-call(bf16[64,256]{1,0:T(8,128)(2,1)} %get-tuple-element.16.dx, bf16[2,256,1024]{2,1,0:T(8,128)(2,1)} %get-tuple-element.17.gin, ...), custom_call_target="tpu_custom_call" | custom-call | tf_op jit(solution)/shard_map/pallas_call | solution.py:711

commit v2 on v1

--- a/solution.py
+++ b/solution.py
@@ -25,6 +25,7 @@
 SMALL = 64
 NX, NY, NZ = 4, 4, 8
 VMEM_BYTES = 60 * 1024 * 1024
+SHORT = ()
 
 
 def dot(a, b, da=1, db=0):
@@ -138,11 +139,11 @@
     n,
     xin, cot, so_in, sf_in, cf_in, cl_in, dk_in, ng_in, ls_in, win_in, wout_in,
     dx_out, gin_out, gout_out, small_s,
-    g_s, r1, g2, r2, g3, r3, ag, sm, sr0, s0, sr1, s1, sr2, s2, sr3, s3,
+    r1, g2, r2, g3, r3, rz, ag, sm, sr0, s0, sr1, s1, sr2, s2, sr3, s3,
     so, sf, cf, cl, x_s, x0_s, cot_s, s0_m, dk_s, ng_s, ls_s,
     win, wout, pk, s_m, st_m, p_m, pt_m,
     pad, dpad, normed_s, inv_s, mixed_s, before_s, slope_s,
-    u_s, h_s, dm_s, db_s, pa, pb,
+    u_s, h_s, dm_s, db_s, a_s, b_s,
     send_f, recv_f, send_b, recv_b,
     wsem, wsend, pksem, fs_sem, fr_sem, bs_sem, br_sem, psend, precv,
     ms_sem, mr_sem, go_sem, ss_sem, sr_sem, so_sem, in_sem, xr_sem,
@@ -200,7 +201,7 @@
     partners += [(other, peer2(d)[1]) for d in range(1, NX)]
     partners += [(seg, peer3(d)[1]) for d in range(1, NZ)]
     for off in OFFSETS:
-        if abs(off) != GW:
+        if abs(off) not in (NZ, 3 * NZ):
             partners.append((seg, lax.rem(tile + off + n, n)))
         partners.append((seg, device_of(lax.rem(tile + off + n, n))))
     partners.append((other, me))
@@ -211,7 +212,7 @@
     def _():
         pl.semaphore_signal(barrier, inc=1, device_id=(seg, mirror), device_id_type=MESH)
 
-    stays = {off: tile == lax.rem(me - off + n, n) for off in (-GW, GW)}
+    stays = {off: tile == lax.rem(me - off + n, n) for off in OFFSETS if abs(off) in (NZ, 3 * NZ)}
     signals = len(partners) + odd
     for off, stay in stays.items():
         signals = signals + jnp.where(stay, 0, 1)
@@ -246,10 +247,16 @@
 
     pl.semaphore_wait(barrier, signals)
 
+    first = [device_of(lax.rem(me - off + n, n)) for off in OFFSETS]
+    behind = [device_of(lax.rem(tile - off + n, n)) for off in OFFSETS]
+    ahead = [device_of(lax.rem(tile + off + n, n)) for off in OFFSETS]
+
     def exchange(src, dst, ssem, rsem, sign, home):
         for slot in SEND_ORDER:
             off = OFFSETS[slot]
             rows = pl.ds(BASE[slot], ROWS[slot])
+
+            to = ahead[slot] if sign < 0 else behind[slot] if home is tile else first[slot]
 
             def go():
                 pltpu.make_async_remote_copy(
@@ -257,7 +264,7 @@
                     dst_ref=dst.at[rows],
                     send_sem=ssem,
                     recv_sem=rsem,
-                    device_id=(seg, device_of(lax.rem(home - sign * off + n, n))),
+                    device_id=(seg, to),
                     device_id_type=MESH,
                 ).start()
 
@@ -293,6 +300,35 @@
 
     pk_copy = to_partner(pk.at[mine], pk.at[mine], pksem.at[0], pksem.at[1])
     pk_copy.start()
+    def operands(b, which):
+        src, dst = ((u_s, h_s), (dm_s, db_s))[which], (a_s, b_s)[which]
+        for kind in range(2):
+            at = (x, y)[kind]
+            whole = (kind == 0) == (which == 0)
+            for d in range(NX):
+                to = lax.rem(at + d, NX)
+                t = me + (to - at) * (NY * NZ, NZ)[kind]
+                part = src[0].at[b] if whole else src[1].at[b, to]
+                slot = dst.at[b, 2 * at + seg]
+
+                def go():
+                    send(part, slot, psend.at[which, b], precv.at[which, b], (kind, t))
+
+                if d > 0:
+                    go()
+                else:
+                    pl.when(seg != kind)(go)
+
+                    @pl.when(seg == kind)
+                    def _():
+                        pltpu.make_async_copy(part, slot, precv.at[which, b]).start()
+
+    def send(src, dst, ssem, rsem, device):
+        pltpu.make_async_remote_copy(
+            src_ref=src, dst_ref=dst, send_sem=ssem, recv_sem=rsem,
+            device_id=device, device_id_type=MESH,
+        ).start()
+
     w_copies = []
     for l in range(2):
         b = 2 * seg + l
@@ -314,23 +350,14 @@
     q1, q2, q3 = 2048 // NX, 2048 // NX // NX, 2048 // NX // NX // NZ
     w1 = 64 // NX
 
-    def send(src, dst, ssem, rsem, device):
-        pltpu.make_async_remote_copy(
-            src_ref=src, dst_ref=dst, send_sem=ssem, recv_sem=rsem,
-            device_id=device, device_id_type=MESH,
-        ).start()
-
     def main_chain(b):
         l, owner = b % 2, b // 2
-        for d in range(1, NX):
-            to, t = peer1(d)
-            send(g_s.at[b, pl.ds(to * q1, q1)], r1.at[b, d - 1], ms_sem.at[0, b], mr_sem.at[0, b], (seg, t))
         yield
-        whole_wait(r1.at[b], mr_sem.at[0, b])
-        total = g_s[b, pl.ds(at1 * q1, q1), :].astype(F32)
-        for d in range(NX - 1):
-            total = total + r1[b, d].astype(F32)
-        g2[b] = total.astype(BF16)
+        for which, ref in ((0, a_s), (1, b_s)):
+            whole_wait(ref.at[b], precv.at[which, b])
+        total = dot(a_s[b].reshape(128 * NX, C), b_s[b].reshape(128 * NX, C), 0, 0)
+        for j in range(2):
+            g2[b, C * j : C * j + C, :] = total[:, 128 * j : 128 * j + 128].astype(BF16)
         for d in range(1, NX):
             to, t = peer2(d)
             send(g2.at[b, pl.ds(to * q2, q2)], r2.at[b, d - 1], ms_sem.at[1, b], mr_sem.at[1, b], (seg, t))
@@ -340,21 +367,31 @@
         for d in range(NX - 1):
             total = total + r2[b, d].astype(F32)
         g3[b] = total.astype(BF16)
-        for d in range(1, NZ):
-            to, t = peer3(d)
-            send(g3.at[b, pl.ds(to * q3, q3)], r3.at[b, d - 1], ms_sem.at[2, b], mr_sem.at[2, b], (seg, t))
-        yield
-        whole_wait(r3.at[b], mr_sem.at[2, b])
-        total = g3[b, pl.ds(z * q3, q3), :].astype(F32)
-        for d in range(NZ - 1):
-            total = total + r3[b, d].astype(F32)
-        here = pl.ds(at2 * q2 + z * q3, q3)
-        ag[b, here, :] = total.astype(BF16)
-        for d in range(1, NZ):
-            send(ag.at[b, here], ag.at[b, here], ms_sem.at[3, b], mr_sem.at[3, b], (seg, peer3(d)[1]))
-        yield
-        whole_wait(ag.at[b, pl.ds(0, (NZ - 1) * q3)], mr_sem.at[3, b])
         here2 = pl.ds(at2 * q2, q2)
+        if b in SHORT:
+            for d in range(1, NZ):
+                send(g3.at[b], rz.at[b, d - 1], ms_sem.at[2, b], mr_sem.at[2, b], (seg, peer3(d)[1]))
+            yield
+            whole_wait(rz.at[b], mr_sem.at[2, b])
+            total = g3[b].astype(F32)
+            for d in range(NZ - 1):
+                total = total + rz[b, d].astype(F32)
+            ag[b, here2, :] = total.astype(BF16)
+        else:
+            for d in range(1, NZ):
+                to, t = peer3(d)
+                send(g3.at[b, pl.ds(to * q3, q3)], r3.at[b, d - 1], ms_sem.at[2, b], mr_sem.at[2, b], (seg, t))
+            yield
+            whole_wait(r3.at[b], mr_sem.at[2, b])
+            total = g3[b, pl.ds(z * q3, q3), :].astype(F32)
+            for d in range(NZ - 1):
+                total = total + r3[b, d].astype(F32)
+            here = pl.ds(at2 * q2 + z * q3, q3)
+            ag[b, here, :] = total.astype(BF16)
+            for d in range(1, NZ):
+                send(ag.at[b, here], ag.at[b, here], ms_sem.at[3, b], mr_sem.at[3, b], (seg, peer3(d)[1]))
+            yield
+            whole_wait(ag.at[b, pl.ds(0, (NZ - 1) * q3)], mr_sem.at[3, b])
         for d in range(1, NX):
             send(ag.at[b, here2], ag.at[b, here2], ms_sem.at[4, b], mr_sem.at[4, b], (seg, peer2(d)[1]))
         yield
@@ -363,16 +400,14 @@
 
             @pl.when(seg == kind)
             def _():
-                if kind == 0:
-                    first = pl.multiple_of(at1 * (q1 // 2), 128)
-                    pairs = [
-                        (ag.at[b, pl.ds(256 * j, 256)], gin_out.at[l, :, pl.ds(first + 128 * j, 128)])
-                        for j in range(q1 // 256)
-                    ]
-                else:
-                    rows = pl.multiple_of(lax.rem(at1 * q1, 1024), 16)
-                    column = pl.multiple_of((at1 * q1 // 1024) * 128, 128)
-                    pairs = [(ag.at[b], gout_out.at[l, pl.ds(rows, q1), pl.ds(column, 128)])]
+                at = pl.multiple_of(at1 * C, 128)
+                pairs = []
+                for j in range(2):
+                    if kind == 0:
+                        dst = gin_out.at[l, :, pl.ds(at + 128 * j, 128)]
+                    else:
+                        dst = gout_out.at[l, pl.ds(at, C), pl.ds(128 * j, 128)]
+                    pairs.append((ag.at[b, pl.ds(C * j, C)], dst))
                 for d in range(1, NX):
                     for src, dst in pairs:
                         send(src, dst, ms_sem.at[5, b], go_sem.at[l, kind], (owner, peer1(d)[1]))
@@ -460,19 +495,14 @@
         before = dot(unit, win[b])
         before_s[...] = before
         hidden = (0.5 * before * (1.0 + lax.erf(before * ROOT_HALF))).astype(BF16)
-        h_s[b] = hidden
+        for k in range(NX):
+            h_s[b, k] = hidden[:, k * HID // NX : (k + 1) * HID // NX]
         whole_wait(wout.at[b], wsem.at[1, b])
         mixed = dot(hidden, wout[b])
         mixed_s[b] = mixed
         curb = (cur + pk[b, 50:51, :] * mixed).astype(BF16)
 
-        @pl.when(seg == 0)
-        def _():
-            to_partner(h_s.at[b], pb.at[b], psend.at[0, b], precv.at[1, b]).start()
-
-        @pl.when(seg == 1)
-        def _():
-            to_partner(u_s.at[b], pa.at[b], psend.at[0, b], precv.at[0, b]).start()
+        operands(b, 0)
 
     whole_wait(cot_s, xr_sem.at[1, 1])
     up = cot_s[...].astype(F32)
@@ -481,18 +511,12 @@
         dm = (up * pk[b, 50:51, :]).astype(BF16)
         dm_s[b] = dm
 
-        @pl.when(seg == 0)
-        def _():
-            to_partner(dm_s.at[b], pa.at[b], psend.at[1, b], precv.at[0, b]).start()
-
         d_hidden = dot(dm, wout[b], 1, 1)
         db = (d_hidden * slope_s[b]).astype(BF16)
-        db_s[b] = db
-
-        @pl.when(seg == 1)
-        def _():
-            to_partner(db_s.at[b], pb.at[b], psend.at[1, b], precv.at[1, b]).start()
-
+        for k in range(NX):
+            db_s[b, k] = db[:, k * HID // NX : (k + 1) * HID // NX]
+        if b == 0:
+            operands(b, 1)
         d_unit = dot(db, win[b], 1, 1)
         normed = normed_s[b]
         inv_std = inv_s[b, :, 0:1]
@@ -522,34 +546,10 @@
                     put(tap, jnp.sum(prod, axis=0, keepdims=True))
             begin(small_chain(b))
 
-        def weight_grads():
-            whole_wait(pa.at[b], precv.at[0, b])
-            whole_wait(pb.at[b], precv.at[1, b])
-
-            @pl.when(seg == 0)
-            def _():
-                g = dot(
-                    jnp.concatenate([u_s[b], pa[b]], axis=0),
-                    jnp.concatenate([db_s[b], pb[b]], axis=0), 0, 0,
-                )
-                for j in range(8):
-                    g_s[b, 256 * j : 256 * j + 256, :] = g[:, 128 * j : 128 * j + 128].astype(BF16)
-
-            @pl.when(seg == 1)
-            def _():
-                g = dot(
-                    jnp.concatenate([h_s[b], pb[b]], axis=0),
-                    jnp.concatenate([dm_s[b], pa[b]], axis=0), 0, 0,
-                )
-                for j in range(2):
-                    g_s[b, 1024 * j : 1024 * j + 1024, :] = g[:, 128 * j : 128 * j + 128].astype(BF16)
-
-            begin(main_chain(b))
+        begin(main_chain(b))
 
         if b == 0:
-            weight_grads()
             small_grads()
-        advance(older)
         dpad[...] = jnp.zeros((16, 16, C), F32)
         for q in range(7):
             rows = [None] * 14
@@ -562,10 +562,11 @@
         send_b[b] = dot(pt_m[...], dpad[...].reshape(256, C).astype(BF16)).astype(BF16)
         exchange(send_b.at[b], recv_b.at[b], bs_sem.at[b], br_sem.at[b], -1, tile)
 
+        if b > 0:
+            operands(b, 1)
         advance(older)
         if b > 0:
             small_grads()
-            weight_grads()
         whole_wait(recv_b.at[b], br_sem.at[b])
         back = dot(st_m[...], recv_b[b])
         up = (up + dpad[3:11, 3:11, :].reshape(64, C) + back).astype(BF16)
@@ -586,17 +587,18 @@
         up = up.astype(F32)
 
     while chains:
-        advance()
+        advance(chains[::-1])
     for l in range(2):
         whole_wait(small_s.at[l], so_sem.at[l])
         whole_wait(gin_out.at[l], go_sem.at[l, 0])
         whole_wait(gout_out.at[l], go_sem.at[l, 1])
     whole_wait(dx_out, xr_sem.at[1, 2])
-    stay = jnp.logical_or(stays[-GW], stays[GW])
+    stay = functools.reduce(jnp.logical_or, stays.values())
+    kept = 256 - ROWS[OFFSETS.index(next(iter(stays)))]
 
     @pl.when(stay)
     def _():
-        whole_wait(send_f.at[0, pl.ds(0, 224)], fs_sem.at[0])
+        whole_wait(send_f.at[0, pl.ds(0, kept)], fs_sem.at[0])
 
     @pl.when(jnp.logical_not(stay))
     def _():
@@ -613,10 +615,14 @@
         if b > 0:
             whole_wait(send_f.at[b], fs_sem.at[b])
         whole_wait(send_b.at[b], bs_sem.at[b])
-        whole_wait(r1.at[b], ms_sem.at[0, b])
+        for which in range(2):
+            whole_wait(a_s.at[b, pl.ds(0, 2 * NX - 1)], psend.at[which, b])
         whole_wait(r2.at[b], ms_sem.at[1, b])
-        whole_wait(r3.at[b], ms_sem.at[2, b])
-        whole_wait(r3.at[b], ms_sem.at[3, b])
+        if b in SHORT:
+            whole_wait(rz.at[b], ms_sem.at[2, b])
+        else:
+            whole_wait(r3.at[b], ms_sem.at[2, b])
+            whole_wait(r3.at[b], ms_sem.at[3, b])
         whole_wait(r2.at[b], ms_sem.at[4, b])
         whole_wait(r1.at[b], ms_sem.at[5, b])
         whole_wait(sr0.at[b], ss_sem.at[0, b])
@@ -630,26 +636,43 @@
             whole_wait(ag.at[b], ms_sem.at[6, b])
             whole_wait(s3.at[b], ss_sem.at[5, b])
 
-        @pl.when(seg == 0)
-        def _():
-            whole_wait(h_s.at[b], psend.at[0, b])
-            whole_wait(dm_s.at[b], psend.at[1, b])
-
-        @pl.when(seg == 1)
-        def _():
-            whole_wait(u_s.at[b], psend.at[0, b])
-            whole_wait(db_s.at[b], psend.at[1, b])
-
-
-def finish(factor, dx, gin, gout, small, dx_out, gin_out, gout_out, gk_out, gg_out, gs_out):
-    gin_out[...] = gin[...].astype(F32) * factor
-    gout_out[...] = gout[...].astype(F32) * factor
-    dx_out[...] = dx[...].reshape(dx_out.shape)
+
+def finish(
+    factor, dx, gin, gout, small, dx_out, gin_out, gout_out, gk_out, gg_out, gs_out,
+    in_n, in_w, out_n, out_w, small_n, gk_w, gg_w, gs_w, in_sem, out_sem,
+):
+    loads, stores, stages = [], [], []
+    for src, dst, narrow, wide in ((gin, gin_out, in_n, in_w), (gout, gout_out, out_n, out_w)):
+        rows = src.shape[1] // 2
+        for l in range(2):
+            for h in range(2):
+                part = pl.ds(h * rows, rows)
+                k = len(loads)
+                loads.append(pltpu.make_async_copy(src.at[l, part], narrow.at[l, part], in_sem.at[k]))
+                stores.append(pltpu.make_async_copy(wide.at[l, part], dst.at[l, part], out_sem.at[k]))
+                stages.append((narrow, wide, l, part))
+    first = pltpu.make_async_copy(small, small_n, in_sem.at[8])
+    pass_on = pltpu.make_async_copy(dx, dx_out, in_sem.at[9])
+    for load in (*loads[:1], first, *loads[1:], pass_on):
+        load.start()
+    for load, store, (narrow, wide, l, part) in zip(loads, stores, stages):
+        load.wait()
+        wide[l, part] = narrow[l, part].astype(F32) * factor
+        store.start()
+    first.wait()
     for l in range(2):
-        total = jnp.concatenate([small[l, 0:64, :], small[l, 64:128, :]], axis=1) * factor
-        gk_out[:, l, :] = total[0:49]
-        gg_out[l : l + 1, :] = total[49:50]
-        gs_out[l : l + 1, :] = total[50:51]
+        total = jnp.concatenate([small_n[l, 0:64, :], small_n[l, 64:128, :]], axis=1) * factor
+        gk_w[:, l, :] = total[0:49]
+        gg_w[l : l + 1, :] = total[49:50]
+        gs_w[l : l + 1, :] = total[50:51]
+    last = [
+        pltpu.make_async_copy(src, dst, out_sem.at[8 + k])
+        for k, (src, dst) in enumerate(((gk_w, gk_out), (gg_w, gg_out), (gs_w, gs_out)))
+    ]
+    for copy in last:
+        copy.start()
+    for copy in (*stores, *last, pass_on):
+        copy.wait()
 
 
 def local(
@@ -674,8 +697,9 @@
         in_specs=[hbm] * 11,
         out_specs=(hbm,) * 4,
         scratch_shapes=[
-            V((BLOCKS, 2048, 128), BF16), V((BLOCKS, NX - 1, q1, 128), BF16), V((BLOCKS, q1, 128), BF16),
+            V((BLOCKS, NX - 1, q1, 128), BF16), V((BLOCKS, q1, 128), BF16),
             V((BLOCKS, NX - 1, q2, 128), BF16), V((BLOCKS, q2, 128), BF16), V((BLOCKS, NZ - 1, q3, 128), BF16),
+            V((BLOCKS, NZ - 1, q2, 128), BF16),
             V((BLOCKS, q1, 128), BF16), V((BLOCKS, 128, 128), F32),
             V((BLOCKS, 64, 128), F32), V((BLOCKS, 64, 128), F32),
             V((BLOCKS, NX - 1, w1, 128), F32), V((BLOCKS, w1, 128), F32),
@@ -689,9 +713,9 @@
             V((BLOCKS, 16, 16, C), F32), V((16, 16, C), F32),
             V((BLOCKS, 64, C), F32), V((BLOCKS, 64, 128), F32), V((BLOCKS, 64, C), F32),
             V((64, HID), F32), V((BLOCKS, 64, HID), F32),
-            V((BLOCKS, 64, C), BF16), V((BLOCKS, 64, HID), BF16),
-            V((BLOCKS, 64, C), BF16), V((BLOCKS, 64, HID), BF16),
-            V((BLOCKS, 64, C), BF16), V((BLOCKS, 64, HID), BF16),
+            V((BLOCKS, 64, C), BF16), V((BLOCKS, NX, 64, HID // NX), BF16),
+            V((BLOCKS, 64, C), BF16), V((BLOCKS, NX, 64, HID // NX), BF16),
+            V((BLOCKS, 2 * NX, 64, C), BF16), V((BLOCKS, 2 * NX, 64, C), BF16),
             V((BLOCKS, 256, C), BF16), V((BLOCKS, 256, C), BF16),
             V((BLOCKS, 256, C), BF16), V((BLOCKS, 256, C), BF16),
             dma((2, BLOCKS)), dma((2, 2)), dma((2,)),
@@ -710,27 +734,19 @@
     )
     dx, d_in, d_out, d_kernel, d_gain, d_scale = pl.pallas_call(
         functools.partial(finish, factor),
-        grid=(4,),
         out_shape=(
             shape((1, 8, 8, C), BF16), shape((2, C, HID), F32), shape((2, HID, C), F32),
             shape((49, 2, C), F32), shape((2, C), F32), shape((2, C), F32),
         ),
-        in_specs=[
-            pl.BlockSpec((64, C), lambda i: (0, 0)),
-            pl.BlockSpec((2, C // 4, HID), lambda i: (0, i, 0)),
-            pl.BlockSpec((2, HID // 4, C), lambda i: (0, i, 0)),
-            pl.BlockSpec((2, 128, 128), lambda i: (0, 0, 0)),
+        in_specs=[hbm] * 4,
+        out_specs=(hbm,) * 6,
+        scratch_shapes=[
+            V((2, C, HID), BF16), V((2, C, HID), F32), V((2, HID, C), BF16), V((2, HID, C), F32),
+            V((2, 128, 128), F32), V((49, 2, C), F32), V((2, C), F32), V((2, C), F32),
+            dma((10,)), dma((11,)),
         ],
-        out_specs=(
-            pl.BlockSpec((1, 8, 8, C), lambda i: (0, 0, 0, 0)),
-            pl.BlockSpec((2, C // 4, HID), lambda i: (0, i, 0)),
-            pl.BlockSpec((2, HID // 4, C), lambda i: (0, i, 0)),
-            pl.BlockSpec((49, 2, C), lambda i: (0, 0, 0)),
-            pl.BlockSpec((2, C), lambda i: (0, 0)),
-            pl.BlockSpec((2, C), lambda i: (0, 0)),
-        ),
         compiler_params=pltpu.CompilerParams(vmem_limit_bytes=VMEM_BYTES),
-    )(dx, d_in, d_out, small)
+    )(dx.reshape(1, 8, 8, C), d_in, d_out, small)
     return dx, d_kernel.transpose(1, 0, 2), d_gain, d_in, d_out, d_scale
 
 

time: 111 us -> 92.4 us (0.83)
  Pallas kernels: 110 us -> 91.5 us
    pallas_call x1, Pallas kernels: 105 us -> 88.3 us  [local(): pl.pallas_call(functools.partial(kernel, n), out_shape=(shape((64, C), BF...]
    pallas_call x1, Pallas kernels: 4.36 us -> 3.2 us  [local(): pl.pallas_call(functools.partial(finish, factor), out_shape=(shape((1, 8,...]
where the time goes in v2:
time: 92.4 us; the launch traced here: 92.3 us
  Pallas kernels  91.5 us (99%)
    pallas_call x1, Pallas kernels, local(): pl.pallas_call(functools.partial(kernel, n), out_shape=(shape((64, C), BF...  88.3 us
    pallas_call x1, Pallas kernels, local(): pl.pallas_call(functools.partial(finish, factor), out_shape=(shape((1, 8,...  3.2 us

profile of v2, /device:TPU:4, one launch (start us, length us, event | category | flops | bytes accessed | tf_op | source)
XLA Modules:
  0.0 92.3 jit_solution(10497225862551487062)
XLA Ops:
  0.6 88.3 %shard_map.154 = (bf16[64,256]{1,0:T(8,128)(2,1)}, bf16[2,256,1024]{2,1,0:T(8,128)(2,1)}, bf16[2,1024,256]{2,1,0:T(8,128)(2,1)}, f32[2,128,128]{2,1,0:T(8,128)}) custom-call(bf16[2,64,256]{2,1,0:T(8,128)(2,1)} %bitcast.9, bf16[2,64,256]{2,1,0:T(8,128)(2,1)} %bitcast.10, s32[4,128]{1,0:T(4,128)} %bitcast.13, s32[4,128]{1,0:T(4,128)} %bitcast.14, ...), custom_call_target="tpu_custom_call" | custom-call | tf_op jit(solution)/shard_map/pallas_call | solution.py:692
  88.9 3.2 %shard_map.155 = (bf16[1,8,8,256]{3,2,1,0:T(8,128)(2,1)}, f32[2,256,1024]{2,1,0:T(8,128)}, f32[2,1024,256]{2,1,0:T(8,128)}, f32[49,2,256]{2,1,0:T(2,128)}, f32[2,256]{1,0:T(2,128)}, /*index=5*/f32[2,256]{1,0:T(2,128)}) custom-call(bf16[1,8,8,256]{3,2,1,0:T(8,128)(2,1)} %bitcast.12, bf16[2,256,1024]{2,1,0:T(8,128)(2,1)} %get-tuple-element.17.gin, ...), custom_call_target="tpu_custom_call" | custom-call | tf_op jit(solution)/shard_map/pallas_call | solution.py:735

commit v3 on v2

--- a/solution.py
+++ b/solution.py
@@ -25,7 +25,6 @@
 SMALL = 64
 NX, NY, NZ = 4, 4, 8
 VMEM_BYTES = 60 * 1024 * 1024
-SHORT = ()
 
 
 def dot(a, b, da=1, db=0):
@@ -139,9 +138,9 @@
     n,
     xin, cot, so_in, sf_in, cf_in, cl_in, dk_in, ng_in, ls_in, win_in, wout_in,
     dx_out, gin_out, gout_out, small_s,
-    r1, g2, r2, g3, r3, rz, ag, sm, sr0, s0, sr1, s1, sr2, s2, sr3, s3,
+    r1, g2, r2, g3, r3, ag, sm, sr0, s0, sr1, s1, sr2, s2, sr3, s3,
     so, sf, cf, cl, x_s, x0_s, cot_s, s0_m, dk_s, ng_s, ls_s,
-    win, wout, pk, s_m, st_m, p_m, pt_m,
+    win, wout, win_t, wout_t, pk, s_m, st_m, p_m, pt_m,
     pad, dpad, normed_s, inv_s, mixed_s, before_s, slope_s,
     u_s, h_s, dm_s, db_s, a_s, b_s,
     send_f, recv_f, send_b, recv_b,
@@ -368,30 +367,20 @@
             total = total + r2[b, d].astype(F32)
         g3[b] = total.astype(BF16)
         here2 = pl.ds(at2 * q2, q2)
-        if b in SHORT:
-            for d in range(1, NZ):
-                send(g3.at[b], rz.at[b, d - 1], ms_sem.at[2, b], mr_sem.at[2, b], (seg, peer3(d)[1]))
-            yield
-            whole_wait(rz.at[b], mr_sem.at[2, b])
-            total = g3[b].astype(F32)
-            for d in range(NZ - 1):
-                total = total + rz[b, d].astype(F32)
-            ag[b, here2, :] = total.astype(BF16)
-        else:
-            for d in range(1, NZ):
-                to, t = peer3(d)
-                send(g3.at[b, pl.ds(to * q3, q3)], r3.at[b, d - 1], ms_sem.at[2, b], mr_sem.at[2, b], (seg, t))
-            yield
-            whole_wait(r3.at[b], mr_sem.at[2, b])
-            total = g3[b, pl.ds(z * q3, q3), :].astype(F32)
-            for d in range(NZ - 1):
-                total = total + r3[b, d].astype(F32)
-            here = pl.ds(at2 * q2 + z * q3, q3)
-            ag[b, here, :] = total.astype(BF16)
-            for d in range(1, NZ):
-                send(ag.at[b, here], ag.at[b, here], ms_sem.at[3, b], mr_sem.at[3, b], (seg, peer3(d)[1]))
-            yield
-            whole_wait(ag.at[b, pl.ds(0, (NZ - 1) * q3)], mr_sem.at[3, b])
+        for d in range(1, NZ):
+            to, t = peer3(d)
+            send(g3.at[b, pl.ds(to * q3, q3)], r3.at[b, d - 1], ms_sem.at[2, b], mr_sem.at[2, b], (seg, t))
+        yield
+        whole_wait(r3.at[b], mr_sem.at[2, b])
+        total = g3[b, pl.ds(z * q3, q3), :].astype(F32)
+        for d in range(NZ - 1):
+            total = total + r3[b, d].astype(F32)
+        here = pl.ds(at2 * q2 + z * q3, q3)
+        ag[b, here, :] = total.astype(BF16)
+        for d in range(1, NZ):
+            send(ag.at[b, here], ag.at[b, here], ms_sem.at[3, b], mr_sem.at[3, b], (seg, peer3(d)[1]))
+        yield
+        whole_wait(ag.at[b, pl.ds(0, (NZ - 1) * q3)], mr_sem.at[3, b])
         for d in range(1, NX):
             send(ag.at[b, here2], ag.at[b, here2], ms_sem.at[4, b], mr_sem.at[4, b], (seg, peer2(d)[1]))
         yield
@@ -469,11 +458,16 @@
             + before * jnp.exp(-0.5 * before * before) * INV_ROOT_TAU
         )
 
+    def turn(b):
+        win_t[b] = jnp.transpose(win[b])
+        wout_t[b] = jnp.transpose(wout[b])
+
     for b in range(BLOCKS):
         if b > 0:
             send_f[b] = dot(s_m[...], curb).astype(BF16)
             exchange(send_f.at[b], recv_f.at[b], fs_sem.at[b], fr_sem.at[b], 1, tile)
             slope_of(b - 1)
+            turn(b - 1)
         cur = curb.astype(F32)
         whole_wait(recv_f.at[b], fr_sem.at[b])
         pad[b] = dot(p_m[...], recv_f[b]).reshape(16, 16, C)
@@ -511,13 +505,13 @@
         dm = (up * pk[b, 50:51, :]).astype(BF16)
         dm_s[b] = dm
 
-        d_hidden = dot(dm, wout[b], 1, 1)
+        d_hidden = dot(dm, wout_t[b]) if b < BLOCKS - 1 else dot(dm, wout[b], 1, 1)
         db = (d_hidden * slope_s[b]).astype(BF16)
         for k in range(NX):
             db_s[b, k] = db[:, k * HID // NX : (k + 1) * HID // NX]
         if b == 0:
             operands(b, 1)
-        d_unit = dot(db, win[b], 1, 1)
+        d_unit = dot(db, win_t[b]) if b < BLOCKS - 1 else dot(db, win[b], 1, 1)
         normed = normed_s[b]
         inv_std = inv_s[b, :, 0:1]
         dn = d_unit * pk[b, 49:50, :]
@@ -618,11 +612,8 @@
         for which in range(2):
             whole_wait(a_s.at[b, pl.ds(0, 2 * NX - 1)], psend.at[which, b])
         whole_wait(r2.at[b], ms_sem.at[1, b])
-        if b in SHORT:
-            whole_wait(rz.at[b], ms_sem.at[2, b])
-        else:
-            whole_wait(r3.at[b], ms_sem.at[2, b])
-            whole_wait(r3.at[b], ms_sem.at[3, b])
+        whole_wait(r3.at[b], ms_sem.at[2, b])
+        whole_wait(r3.at[b], ms_sem.at[3, b])
         whole_wait(r2.at[b], ms_sem.at[4, b])
         whole_wait(r1.at[b], ms_sem.at[5, b])
         whole_wait(sr0.at[b], ss_sem.at[0, b])
@@ -699,7 +690,6 @@
         scratch_shapes=[
             V((BLOCKS, NX - 1, q1, 128), BF16), V((BLOCKS, q1, 128), BF16),
             V((BLOCKS, NX - 1, q2, 128), BF16), V((BLOCKS, q2, 128), BF16), V((BLOCKS, NZ - 1, q3, 128), BF16),
-            V((BLOCKS, NZ - 1, q2, 128), BF16),
             V((BLOCKS, q1, 128), BF16), V((BLOCKS, 128, 128), F32),
             V((BLOCKS, 64, 128), F32), V((BLOCKS, 64, 128), F32),
             V((BLOCKS, NX - 1, w1, 128), F32), V((BLOCKS, w1, 128), F32),
@@ -708,7 +698,8 @@
             S((4, n), jnp.int32), S((4, n), jnp.int32), S((4, n), jnp.int32), S((4, n), jnp.int32),
             V((64, C), BF16), V((64, C), BF16), V((64, C), BF16), V((256, 64), BF16),
             V((49, 2, C), BF16), V((2, C), F32), V((2, C), F32),
-            V((BLOCKS, C, HID), BF16), V((BLOCKS, HID, C), BF16), V((BLOCKS, SMALL, C), F32),
+            V((BLOCKS, C, HID), BF16), V((BLOCKS, HID, C), BF16),
+            V((BLOCKS - 1, HID, C), BF16), V((BLOCKS - 1, C, HID), BF16), V((BLOCKS, SMALL, C), F32),
             V((256, 64), BF16), V((64, 256), BF16), V((256, 256), BF16), V((256, 256), BF16),
             V((BLOCKS, 16, 16, C), F32), V((16, 16, C), F32),
             V((BLOCKS, 64, C), F32), V((BLOCKS, 64, 128), F32), V((BLOCKS, 64, C), F32),

time: 92.4 us -> 91.8 us (level)
  no operation moved by 1% of the time
where the time goes in v3:
time: 91.8 us; the launch traced here: 91.4 us
  Pallas kernels  90.6 us (99%)
    pallas_call x1, Pallas kernels, local(): pl.pallas_call(functools.partial(kernel, n), out_shape=(shape((64, C), BF...  87.4 us
    pallas_call x1, Pallas kernels, local(): pl.pallas_call(functools.partial(finish, factor), out_shape=(shape((1, 8,...  3.2 us

profile of v3, /device:TPU:4, one launch (start us, length us, event | category | flops | bytes accessed | tf_op | source)
XLA Modules:
  0.0 91.4 jit_solution(16478485779073080153)
XLA Ops:
  0.6 87.4 %shard_map.154 = (bf16[64,256]{1,0:T(8,128)(2,1)}, bf16[2,256,1024]{2,1,0:T(8,128)(2,1)}, bf16[2,1024,256]{2,1,0:T(8,128)(2,1)}, f32[2,128,128]{2,1,0:T(8,128)}) custom-call(bf16[2,64,256]{2,1,0:T(8,128)(2,1)} %bitcast.9, bf16[2,64,256]{2,1,0:T(8,128)(2,1)} %bitcast.10, s32[4,128]{1,0:T(4,128)} %bitcast.13, s32[4,128]{1,0:T(4,128)} %bitcast.14, ...), custom_call_target="tpu_custom_call" | custom-call | tf_op jit(solution)/shard_map/pallas_call | solution.py:683
  88.0 3.2 %shard_map.155 = (bf16[1,8,8,256]{3,2,1,0:T(8,128)(2,1)}, f32[2,256,1024]{2,1,0:T(8,128)}, f32[2,1024,256]{2,1,0:T(8,128)}, f32[49,2,256]{2,1,0:T(2,128)}, f32[2,256]{1,0:T(2,128)}, /*index=5*/f32[2,256]{1,0:T(2,128)}) custom-call(bf16[1,8,8,256]{3,2,1,0:T(8,128)(2,1)} %bitcast.12, bf16[2,256,1024]{2,1,0:T(8,128)(2,1)} %get-tuple-element.17.gin, ...), custom_call_target="tpu_custom_call" | custom-call | tf_op jit(solution)/shard_map/pallas_call | solution.py:726

commit v4 on v3

--- a/solution.py
+++ b/solution.py
@@ -145,7 +145,7 @@
     u_s, h_s, dm_s, db_s, a_s, b_s,
     send_f, recv_f, send_b, recv_b,
     wsem, wsend, pksem, fs_sem, fr_sem, bs_sem, br_sem, psend, precv,
-    ms_sem, mr_sem, go_sem, ss_sem, sr_sem, so_sem, in_sem, xr_sem,
+    ms_sem, mr_sem, go_sem, ss_sem, sr_sem, so_sem, in_sem, xr_sem, gp_sem,
 ):
     seg = lax.axis_index("segment")
     me = lax.axis_index("tile")
@@ -349,6 +349,27 @@
     q1, q2, q3 = 2048 // NX, 2048 // NX // NX, 2048 // NX // NX // NZ
     w1 = 64 // NX
 
+    def deliver(b, block):
+        l, owner = b % 2, b // 2
+        row = pl.multiple_of(lax.rem(block, 2) * 128, 128)
+        column = pl.multiple_of((block // 2) * 128, 128)
+        base = pl.multiple_of(at1 * C, 128)
+        src = ag.at[b, pl.ds(block * q2, q2)]
+        for kind in range(2):
+
+            @pl.when(seg == kind)
+            def _():
+                if kind == 0:
+                    dst = gin_out.at[l, pl.ds(row, 128), pl.ds(base + column, 128)]
+                else:
+                    dst = gout_out.at[l, pl.ds(base + row, 128), pl.ds(column, 128)]
+                for d in range(1, NX):
+                    send(src, dst, ms_sem.at[5, b], go_sem.at[l, kind], (owner, peer1(d)[1]))
+                if kind == owner:
+                    pltpu.make_async_copy(src, dst, go_sem.at[l, kind]).start()
+                else:
+                    send(src, dst, ms_sem.at[6, b], go_sem.at[l, kind], (other, me))
+
     def main_chain(b):
         l, owner = b % 2, b // 2
         yield
@@ -382,8 +403,17 @@
         yield
         whole_wait(ag.at[b, pl.ds(0, (NZ - 1) * q3)], mr_sem.at[3, b])
         for d in range(1, NX):
-            send(ag.at[b, here2], ag.at[b, here2], ms_sem.at[4, b], mr_sem.at[4, b], (seg, peer2(d)[1]))
-        yield
+            arrived = gp_sem.at[d - 1] if b == 0 else mr_sem.at[4, b]
+            send(ag.at[b, here2], ag.at[b, here2], ms_sem.at[4, b], arrived, (seg, peer2(d)[1]))
+        if b == 0:
+            deliver(b, at2)
+        yield
+        if b == 0:
+            for d in (1, 3, 2):
+                block = lax.rem(at2 - d + NX, NX)
+                whole_wait(ag.at[b, pl.ds(block * q2, q2)], gp_sem.at[d - 1])
+                deliver(b, block)
+            return
         whole_wait(ag.at[b, pl.ds(0, (NX - 1) * q2)], mr_sem.at[4, b])
         for kind in range(2):
 
@@ -713,7 +743,7 @@
             dma((BLOCKS,)), dma((BLOCKS,)), dma((BLOCKS,)), dma((BLOCKS,)),
             dma((2, BLOCKS)), dma((2, BLOCKS)),
             dma((7, BLOCKS)), dma((5, BLOCKS)), dma((2, 2)), dma((6, BLOCKS)), dma((4, BLOCKS)), dma((2,)),
-            dma((8,)), dma((2, 3)),
+            dma((8,)), dma((2, 3)), dma((3,)),
         ],
         compiler_params=pltpu.CompilerParams(
             collective_id=0, has_side_effects=True, vmem_limit_bytes=VMEM_BYTES

time: 91.8 us -> 91.9 us (level)
  no operation moved by 1% of the time
where the time goes in v4:
time: 91.9 us; the launch traced here: 90.8 us
  Pallas kernels  90 us (98%)
    pallas_call x1, Pallas kernels, local(): pl.pallas_call(functools.partial(kernel, n), out_shape=(shape((64, C), BF...  86.8 us
    pallas_call x1, Pallas kernels, local(): pl.pallas_call(functools.partial(finish, factor), out_shape=(shape((1, 8,...  3.2 us

profile of v4, /device:TPU:4, one launch (start us, length us, event | category | flops | bytes accessed | tf_op | source)
XLA Modules:
  0.0 90.8 jit_solution(18398517353106402310)
XLA Ops:
  0.6 86.8 %shard_map.154 = (bf16[64,256]{1,0:T(8,128)(2,1)}, bf16[2,256,1024]{2,1,0:T(8,128)(2,1)}, bf16[2,1024,256]{2,1,0:T(8,128)(2,1)}, f32[2,128,128]{2,1,0:T(8,128)}) custom-call(bf16[2,64,256]{2,1,0:T(8,128)(2,1)} %bitcast.9, bf16[2,64,256]{2,1,0:T(8,128)(2,1)} %bitcast.10, s32[4,128]{1,0:T(4,128)} %bitcast.13, s32[4,128]{1,0:T(4,128)} %bitcast.14, ...), custom_call_target="tpu_custom_call" | custom-call | tf_op jit(solution)/shard_map/pallas_call | solution.py:713
  87.4 3.2 %shard_map.155 = (bf16[1,8,8,256]{3,2,1,0:T(8,128)(2,1)}, f32[2,256,1024]{2,1,0:T(8,128)}, f32[2,1024,256]{2,1,0:T(8,128)}, f32[49,2,256]{2,1,0:T(2,128)}, f32[2,256]{1,0:T(2,128)}, /*index=5*/f32[2,256]{1,0:T(2,128)}) custom-call(bf16[1,8,8,256]{3,2,1,0:T(8,128)(2,1)} %bitcast.12, bf16[2,256,1024]{2,1,0:T(8,128)(2,1)} %get-tuple-element.17.gin, ...), custom_call_target="tpu_custom_call" | custom-call | tf_op jit(solution)/shard_map/pallas_call | solution.py:756
